TPU v7x, 32 devices: a whole 2x2x4 slice. The times are simulated.
32 devices in a mesh: depth: 16 (over z, y, x), slab: 2 (over core).
Axes of the slice: x: 2, y: 2, z: 4, core: 2. Of those that a mesh axis runs over, the one named last changes fastest.
Arguments:
- ref_feat: bfloat16 [4, 32, 128], P('slab'), may hold values from -9 to 9
- src_feat: bfloat16 [2560, 32, 128], P('depth'), may hold values from -9 to 9
- tile_owner: int32 [1280, 1], P(('depth', 'slab')), may hold values from 0 to 15; in each aligned block of 40 rows (0 to 39, 40 to 79, ...) at most 4 rows name the same one
- tile_local: int32 [1280], P(('depth', 'slab')), may hold values from 0 to 159
- col_shift: int32 [1280], P(('depth', 'slab')), may hold values from -16 to 16
- w_gates: bfloat16 [9, 64, 8], replicated, may hold values from -1.4375 to 1.4375
- bias_z: float32 [32], replicated
- bias_c: float32 [32], replicated, may hold values from -3 to 3
- w_out: float32 [32], replicated
Outputs:
- probability: float32 [64, 4, 128], P('depth', 'slab')
- depth_map: float32 [4, 128], P('slab')
Inputs may be any that keep to these rules, and one draw needn't show every extreme that they name: `tile_owner`: among the requests of one device no owner is named more than 4 times; in some devices one owner is named exactly 4 times.
All inputs are finite; a program needn't handle non-finite values.
Results may differ from a plain program's by a relative error of at most 0.00085.
Values may be sent and summed in bfloat16 or wider, within the bound.
A program may use at most 64 MiB of HBM per device.

v0:
```python
import jax
import jax.numpy as jnp
from jax import lax
from jax.sharding import PartitionSpec as P

VIEWS = 5
PD = 4


def padded_2(cells, sides, width):
    for axis, dim in sides:
        count = lax.axis_size(axis)
        ends = count - 1
        head = lax.slice_in_dim(cells, 0, width, axis=dim)
        tail = lax.slice_in_dim(cells, cells.shape[dim] - width, cells.shape[dim], axis=dim)
        cells = jnp.concatenate(
            [
                lax.ppermute(tail, axis, [(i, (i + 1) % count) for i in range(ends)]),
                cells,
                lax.ppermute(head, axis, [((i + 1) % count, i) for i in range(ends)]),
            ],
            axis=dim,
        )
    return cells


def prefix_2(shard, axis, combine, identity):
    count, index = (lax.axis_size(axis), lax.axis_index(axis))
    everything = jax.tree.map(lambda part: lax.all_gather(part, axis), shard)
    start = jax.tree.map(
        lambda part, zero: jnp.broadcast_to(jnp.asarray(zero, part.dtype), part.shape),
        shard,
        identity,
    )

    def turn(k, before):
        reached = k < index
        new = combine(before, jax.tree.map(lambda part: part[k], everything))
        return jax.tree.map(lambda a, b: jnp.where(reached, a, b), new, before)

    return lax.fori_loop(0, count, turn, start)


def warp_tiles(tile_rows, shift_cols):
    col_count = tile_rows.shape[-1]
    positions = jnp.arange(col_count, dtype=jnp.int32)
    source_col = positions[None, :] - shift_cols[..., None, None]
    selector = (positions[:, None] == source_col).astype(tile_rows.dtype)
    moved = jnp.einsum(
        "...cy,...yx->...cx", tile_rows, selector, preferred_element_type=jnp.float32
    )
    return moved.astype(tile_rows.dtype)


def correlate(warped, ref_rows, groups):
    leading = warped.shape[:-2]
    feat_count = warped.shape[-2]
    col_count = warped.shape[-1]
    split_shape = leading + (groups, feat_count // groups, col_count)
    product = warped.astype(jnp.float32) * ref_rows.astype(jnp.float32)
    return jnp.sum(product.reshape(split_shape), axis=-2)


def body(ref_feat, src_feat, tile_owner, tile_local, col_shift, w_gates, bias_z, bias_c, w_out):
    owners = lax.axis_size("depth")
    row_count, feat_count, col_count = ref_feat.shape
    groups = w_gates.shape[2]
    hidden = w_gates.shape[1] // 2
    requests = tile_owner.shape[0]
    capacity = max(2, (3 * requests + 2 * owners - 1) // (2 * owners))
    owner_of = tile_owner[:, 0]
    onehot = (owner_of[:, None] == jnp.arange(owners, dtype=jnp.int32)[None, :]).astype(jnp.int32)
    slot_of = jnp.sum((jnp.cumsum(onehot, axis=0) - onehot) * onehot, axis=1)
    empty_ids = jnp.zeros((owners, capacity), jnp.int32)
    send_ids = empty_ids.at[owner_of, slot_of].set(tile_local)
    ref_rows = jnp.broadcast_to(
        ref_feat[None, None], (PD, VIEWS, row_count, feat_count, col_count)
    ).reshape(requests, feat_count, col_count)
    send_shift = empty_ids.at[owner_of, slot_of].set(col_shift)
    send_rows = (
        jnp.zeros((owners, capacity, feat_count, col_count), jnp.bfloat16)
        .at[owner_of, slot_of]
        .set(ref_rows)
    )
    slot_ids = lax.all_to_all(send_ids, "depth", split_axis=0, concat_axis=0, tiled=True)
    slot_shift = lax.all_to_all(send_shift, "depth", split_axis=0, concat_axis=0, tiled=True)
    slot_rows = lax.all_to_all(send_rows, "depth", split_axis=0, concat_axis=0, tiled=True)
    tile_rows = jnp.take(src_feat, slot_ids, axis=0)
    group_terms = correlate(warp_tiles(tile_rows, slot_shift), slot_rows, groups)
    answers = lax.all_to_all(group_terms, "depth", split_axis=0, concat_axis=0, tiled=True)
    per_request = answers[owner_of, slot_of]
    summed = per_request.reshape(PD, VIEWS, row_count, groups, col_count).sum(axis=1)
    cost = summed / (VIEWS * (feat_count // groups))
    rimmed = padded_2(cost, (("slab", 1),), 1)
    padded = jnp.pad(rimmed, ((0, 0), (0, 0), (0, 0), (1, 1)))
    windows = []
    for tap_index in range(9):
        row_step = tap_index // 3
        col_step = tap_index % 3
        windows.append(
            padded[:, row_step : row_step + row_count, :, col_step : col_step + col_count]
        )
    stacked = (
        jnp.stack(windows).transpose(0, 3, 1, 2, 4).reshape(9 * groups, PD * row_count * col_count)
    )
    gate_matrix = w_gates.astype(jnp.float32).transpose(1, 0, 2).reshape(2 * hidden, 9 * groups)
    preact = jnp.dot(
        gate_matrix, stacked, precision=lax.Precision.HIGHEST, preferred_element_type=jnp.float32
    )
    preact = preact.reshape(2 * hidden, PD, row_count, col_count)
    retain = jax.nn.sigmoid(preact[:hidden] + bias_z[:, None, None, None])
    candidate = jnp.tanh(preact[hidden:] + bias_c[:, None, None, None])
    fresh = (1.0 - retain) * candidate
    decay_all = jnp.ones((hidden, row_count, col_count), jnp.float32)
    offset_all = jnp.zeros((hidden, row_count, col_count), jnp.float32)
    for plane in range(PD):
        decay_all = retain[:, plane] * decay_all
        offset_all = retain[:, plane] * offset_all + fresh[:, plane]

    def combine(earlier, latter):
        return (latter[0] * earlier[0], latter[0] * earlier[1] + latter[1])

    prefix = prefix_2(
        (decay_all, offset_all),
        "depth",
        combine,
        (jnp.ones_like(decay_all), jnp.zeros_like(offset_all)),
    )
    current = prefix[1]
    score_list = []
    for plane in range(PD):
        current = retain[:, plane] * current + fresh[:, plane]
        score_list.append(jnp.sum(current * w_out[:, None, None], axis=0))
    scores = jnp.stack(score_list)
    plane_index = lax.axis_index("depth") * PD + jnp.arange(PD, dtype=jnp.int32)
    depth_value = 1.0 / (0.1 + 0.9 * plane_index.astype(jnp.float32) / (PD * owners - 1))
    local_max = jnp.max(scores, axis=0)
    highest = lax.pmax(local_max, "depth")
    weights = jnp.exp(scores - highest[None])
    totals, depth_sum = lax.psum(
        (jnp.sum(weights, axis=0), jnp.sum(weights * depth_value[:, None, None], axis=0)), "depth"
    )
    probability = weights / totals[None]
    return (probability, depth_sum / totals)


def solution(mesh):
    return jax.shard_map(
        body,
        mesh=mesh,
        in_specs=(
            P("slab", None, None),
            P("depth", None, None),
            P(("depth", "slab"), None),
            P(("depth", "slab")),
            P(("depth", "slab")),
            P(),
            P(),
            P(),
            P(),
        ),
        out_specs=(P("depth", "slab", None), P("slab", None)),
        check_vma=False,
    )
```

profile of v0, /device:TPU:0, one launch (start us, length us, event | category | flops | bytes accessed | tf_op | source)
XLA Modules:
  0.0 235.4 jit_solution(14627007232976816457)
XLA Ops:
  0.7 0.8 fusion.35
  1.6 0.8 select_reduce_fusion
  3.1 4.4 %scatter_fusion = s32[16,4]{0,1:T(4,128)S(1)} fusion(s32[16,4]{0,1:T(4,128)S(1)} %broadcast_in_dim.15.clone.1, s32[40]{0:T(128)S(1)} %get-tuple-element.148, s32[40]{0:T(128)} %param.14), kind=kCustom, calls=%fused_computation.2 | custom fusion | bytes 800 | tf_op jit(solution)/shard_map/scatter | solution.py:75
  8.2 8.3 %all-to-all-start = ((s32[16,1,4]{2,1,0:T(1,128)}), s32[16,1,4]{2,1,0:T(1,128)S(1)}, u32[]{:S(2)}, u32[]{:S(2)}) async-start(s32[16,1,4]{2,1,0:T(1,128)} %copy.34), calls=%async_computation | async-start | bytes 16384 | tf_op jit(solution)/shard_map/all_to_all | solution.py:85
  16.5 4.4 %scatter_fusion.1 = s32[16,4]{0,1:T(4,128)S(1)} fusion(s32[16,4]{0,1:T(4,128)S(1)} %broadcast_in_dim.15.clone, s32[40]{0:T(128)S(1)} %get-tuple-element.148, s32[40]{0:T(128)} %param.15), kind=kCustom, calls=%fused_computation.3 | custom fusion | bytes 800 | tf_op jit(solution)/shard_map/scatter | solution.py:79
  21.7 2.1 all-to-all-done
  23.8 4.8 %all-to-all-start.1 = ((s32[16,1,4]{2,1,0:T(1,128)}), s32[16,1,4]{2,1,0:T(1,128)S(1)}, u32[]{:S(2)}, u32[]{:S(2)}) async-start(s32[16,1,4]{2,1,0:T(1,128)} %copy.39), calls=%async_computation.1 | async-start | bytes 16384 | tf_op jit(solution)/shard_map/all_to_all | solution.py:86
  28.7 0.9 broadcast_in_dim.22
  29.6 5.6 %scatter_fusion.2 = bf16[16,4,32,128]{3,2,1,0:T(8,128)(2,1)} fusion(bf16[16,4,32,128]{3,2,1,0:T(8,128)(2,1)} %broadcast_in_dim.22, s32[40]{0:T(128)S(1)} %get-tuple-element.148, bf16[40,32,128]{2,1,0:T(8,128)(2,1)S(1)} %bitcast.172), kind=kCustom, calls=%fused_computation.4 | custom fusion | bytes 983360 | tf_op jit(solution)/shard_map/scatter | solution.py:83
  35.8 6.2 %all-to-all-start.2 = ((bf16[16,4,32,128]{3,2,1,0:T(8,128)(2,1)}), bf16[16,4,32,128]{3,2,1,0:T(8,128)(2,1)S(1)}, u32[]{:S(2)}, u32[]{:S(2)}) async-start(bf16[16,4,32,128]{3,2,1,0:T(8,128)(2,1)} %scatter_fusion.2), calls=%async_computation.2 | async-start | bytes 1048576 | tf_op jit(solution)/shard_map/all_to_all | solution.py:87
  43.2 12.9 %all-to-all-done.2 = bf16[16,4,32,128]{3,2,1,0:T(8,128)(2,1)S(1)} async-done(((bf16[16,4,32,128]{3,2,1,0:T(8,128)(2,1)}), bf16[16,4,32,128]{3,2,1,0:T(8,128)(2,1)S(1)}, u32[]{:S(2)}, u32[]{:S(2)}) %all-to-all-start.2) | async-done | bytes 524320 | tf_op jit(solution)/shard_map/all_to_all | solution.py:87
  56.1 0.9 fusion.7
  57.1 1.4 reduce_sum.85
  58.5 4.0 %all-to-all-start.3 = ((f32[16,4,8,128]{3,2,1,0:T(8,128)}), f32[16,4,8,128]{3,2,1,0:T(8,128)S(1)}, u32[]{:S(2)}, u32[]{:S(2)}) async-start(f32[16,4,8,128]{3,2,1,0:T(8,128)} %reduce_sum.85), calls=%async_computation.3 | async-start | bytes 524288 | tf_op jit(solution)/shard_map/all_to_all | solution.py:90
  62.4 8.5 %all-to-all-done.3 = f32[16,4,8,128]{3,2,1,0:T(8,128)S(1)} async-done(((f32[16,4,8,128]{3,2,1,0:T(8,128)}), f32[16,4,8,128]{3,2,1,0:T(8,128)S(1)}, u32[]{:S(2)}, u32[]{:S(2)}) %all-to-all-start.3) | async-done | bytes 262176 | tf_op jit(solution)/shard_map/all_to_all | solution.py:90
  70.9 0.8 gather_fusion.1
  71.8 1.3 collective-permute-start
  73.1 1.3 collective-permute-start.1
  74.4 1.7 collective-permute-done.1
  77.3 41.2 %all_gather.8 = f32[16,32,2,128]{3,1,2,0:T(8,128)S(1)} all-gather(f32[1,32,2,128]{3,1,2,0:T(8,128)S(1)} %get-tuple-element.155), channel_id=1, replica_groups=mesh['depth'=16,'slab'=2] {'depth'}, dimensions={0}, use_global_device_ids=true | all-gather | bytes 557056 | tf_op jit(solution)/shard_map/all_gather | solution.py:29
  118.5 38.7 %all_gather.9 = f32[16,32,2,128]{3,1,2,0:T(8,128)S(1)} all-gather(f32[1,32,2,128]{3,1,2,0:T(8,128)S(1)} %get-tuple-element.154), channel_id=1, replica_groups=mesh['depth'=16,'slab'=2] {'depth'}, dimensions={0}, use_global_device_ids=true | all-gather | bytes 557056 | tf_op jit(solution)/shard_map/all_gather | solution.py:29
  157.2 1.7 while.14
  159.0 38.6 %pmax.7 = f32[2,128]{1,0:T(2,128)S(1)} all-reduce(f32[2,128]{1,0:T(2,128)S(1)} %maximum_maximum_fusion), channel_id=1, replica_groups=mesh['depth'=16,'slab'=2] {'depth'}, use_global_device_ids=true, to_apply=%region_13.14 | all-reduce | flops 256 | bytes 2048 | tf_op jit(solution)/shard_map/pmax | solution.py:138
  197.7 36.5 %all-reduce.1 = (f32[2,128]{1,0:T(2,128)S(1)}, f32[2,128]{1,0:T(2,128)S(1)}) all-reduce(f32[2,128]{1,0:T(2,128)S(1)} %get-tuple-element.130, f32[2,128]{1,0:T(2,128)S(1)} %get-tuple-element.129), channel_id=1, replica_groups=mesh['depth'=16,'slab'=2] {'depth'}, use_global_device_ids=true, to_apply=%region_15.16 | all-reduce | flops 512 | bytes 4096 | tf_op jit(solution)/shard_map/psum | solution.py:140
  (90 shorter events, 7.7 us)
Async XLA Ops:
  0.6 41.9 %copy-start = (bf16[160,32,128]{2,1,0:T(8,128)(2,1)S(1)}, bf16[160,32,128]{2,1,0:T(8,128)(2,1)}, u32[]{:S(2)}) copy-start(bf16[160,32,128]{2,1,0:T(8,128)(2,1)} %param.12) | copy-start | bytes 3932164
  0.6 27.9 %copy-start.2 = (bf16[2,32,128]{2,1,0:T(8,128)(2,1)S(1)}, bf16[2,32,128]{2,1,0:T(8,128)(2,1)}, u32[]{:S(2)}) copy-start(bf16[2,32,128]{2,1,0:T(8,128)(2,1)} %param.11) | copy-start | bytes 49156
  8.2 15.6 %all-to-all-start = ((s32[16,1,4]{2,1,0:T(1,128)}), s32[16,1,4]{2,1,0:T(1,128)S(1)}, u32[]{:S(2)}, u32[]{:S(2)}) async-start(s32[16,1,4]{2,1,0:T(1,128)} %copy.34), calls=%async_computation | async-start | bytes 16384 | tf_op jit(solution)/shard_map/all_to_all | solution.py:85
  23.8 12.1 %all-to-all-start.1 = ((s32[16,1,4]{2,1,0:T(1,128)}), s32[16,1,4]{2,1,0:T(1,128)S(1)}, u32[]{:S(2)}, u32[]{:S(2)}) async-start(s32[16,1,4]{2,1,0:T(1,128)} %copy.39), calls=%async_computation.1 | async-start | bytes 16384 | tf_op jit(solution)/shard_map/all_to_all | solution.py:86
  35.8 20.3 %all-to-all-start.2 = ((bf16[16,4,32,128]{3,2,1,0:T(8,128)(2,1)}), bf16[16,4,32,128]{3,2,1,0:T(8,128)(2,1)S(1)}, u32[]{:S(2)}, u32[]{:S(2)}) async-start(bf16[16,4,32,128]{3,2,1,0:T(8,128)(2,1)} %scatter_fusion.2), calls=%async_computation.2 | async-start | bytes 1048576 | tf_op jit(solution)/shard_map/all_to_all | solution.py:87
  58.4 18.1 %copy-start.1 = (bf16[9,64,8]{1,2,0:T(8,128)(2,1)S(1)}, bf16[9,64,8]{1,2,0:T(8,128)(2,1)}, u32[]{:S(2)}) copy-start(bf16[9,64,8]{1,2,0:T(8,128)(2,1)} %param.16) | copy-start | bytes 27652
  58.5 12.5 %all-to-all-start.3 = ((f32[16,4,8,128]{3,2,1,0:T(8,128)}), f32[16,4,8,128]{3,2,1,0:T(8,128)S(1)}, u32[]{:S(2)}, u32[]{:S(2)}) async-start(f32[16,4,8,128]{3,2,1,0:T(8,128)} %reduce_sum.85), calls=%async_computation.3 | async-start | bytes 524288 | tf_op jit(solution)/shard_map/all_to_all | solution.py:90
  71.7 5.4 %copy-start.4 = (f32[32]{0:T(128)S(1)}, f32[32]{0:T(128)}, u32[]{:S(2)}) copy-start(f32[32]{0:T(128)} %param.18) | copy-start | bytes 388
  71.7 5.4 %copy-start.5 = (f32[32]{0:T(128)S(1)}, f32[32]{0:T(128)}, u32[]{:S(2)}) copy-start(f32[32]{0:T(128)} %param.17) | copy-start | bytes 388
  71.8 2.6 %collective-permute-start = (f32[4,1,8,128]{3,2,1,0:T(8,128)S(1)}, f32[4,1,8,128]{3,2,1,0:T(8,128)S(1)}, u32[]{:S(2)}, u32[]{:S(2)}) collective-permute-start(f32[4,1,8,128]{3,2,1,0:T(8,128)S(1)} %get-tuple-element.156), channel_id=1, source_target_pairs={{0,1},{2,3},{4,5},{6,7},{8,9},{10,11},{12,13},{14,15},{16,17},{18,... | collective-permute-start | bytes 49160 | tf_op jit(solution)/shard_map/ppermute | solution.py:18
  73.1 3.1 %collective-permute-start.1 = (f32[4,1,8,128]{3,2,1,0:T(8,128)S(1)}, f32[4,1,8,128]{3,2,1,0:T(8,128)S(1)}, u32[]{:S(2)}, u32[]{:S(2)}) collective-permute-start(f32[4,1,8,128]{3,2,1,0:T(8,128)S(1)} %get-tuple-element.157), channel_id=1, source_target_pairs={{1,0},{3,2},{5,4},{7,6},{9,8},{11,10},{13,12},{15,14},{17,16},{19,... | collective-permute-start | bytes 49160 | tf_op jit(solution)/shard_map/ppermute | solution.py:20
  118.5 40.4 %copy-start.3 = (f32[32]{0:T(128)S(1)}, f32[32]{0:T(128)}, u32[]{:S(2)}) copy-start(f32[32]{0:T(128)} %param.19) | copy-start | bytes 388
where the time goes:
time: 236 us; the launch traced here: 235 us
  blocking collectives  155 us (66%)
  waiting for transfers between devices  26 us (11%)
  starting transfers between devices  25.9 us (11%)
  local copies, waits for them, and re-layouts  19.2 us (8%)
  other arithmetic  6.58 us (3%)
    all_gather x2, blocking collectives, prefix_2(): everything = jax.tree.map(lambda part: lax.all_gather(part, axis), shard)  79.8 us
    pmax x1, blocking collectives, body(): highest = lax.pmax(local_max, 'depth')  38.6 us
    psum x1, blocking collectives, body(): lax.psum((jnp.sum(weights, axis=0), jnp.sum(weights * depth_value[:, None...  36.5 us
    all_to_all x1, waiting for transfers between devices, body(): lax.all_to_all(send_rows, 'depth', split_axis=0, concat_axis=0, tiled=True)  12.9 us
    all_to_all x1, waiting for transfers between devices, body(): lax.all_to_all(group_terms, 'depth', split_axis=0, concat_axis=0, tiled=T...  8.5 us
    all_to_all x1, starting transfers between devices, body(): lax.all_to_all(send_ids, 'depth', split_axis=0, concat_axis=0, tiled=True)  8.31 us
    all_to_all x1, starting transfers between devices, body(): lax.all_to_all(send_rows, 'depth', split_axis=0, concat_axis=0, tiled=True)  6.24 us
    scatter x1, local copies, waits for them, and re-layouts, body(): send_rows = jnp.zeros((owners, capacity, feat_count, col_count), jnp.bflo...  5.57 us
  transfers between devices with their start and end apart: 6, of which 5 were waited for; matrix products, arithmetic and copies ran while one was open for 5% of the time, Pallas kernels for 0%

commit v1 on v0

v1 whole, which is shorter than its diff:
```python
import functools

import jax
import jax.numpy as jnp
from jax import lax
from jax.experimental import pallas as pl
from jax.experimental.pallas import tpu as pltpu
from jax.sharding import PartitionSpec as P

VIEWS = 5
PD = 4
MAXSHIFT = 16
MESH = pl.DeviceIdType.MESH
F32 = jnp.float32
I32 = jnp.int32


def kernel(
    n, cap, seg,
    ref_ref, src_hbm, owner_ref, local_ref, shift_ref, w_ref, bz_ref, bc_ref, wo_ref,
    prob_ref, depth_ref,
    src, ref_wide, tab_send, tab_recv, tab_s, own_v, own_s, prod, ans_send, ans_recv,
    edge_send, edge_recv, win, fwd_send, fwd_recv, back_send, back_recv, stat_send, stat_recv,
    src_sem, smem_sems, send_sems, recv_sems,
):
    me = lax.axis_index("depth")
    slab = lax.axis_index("slab")
    requests = owner_ref.shape[0]
    rows, feat, cols = ref_ref.shape
    groups = w_ref.shape[2]
    hidden = w_ref.shape[1] // 2
    cpg = feat // groups

    def peer(k):
        return lax.rem(me + k, n)

    barrier = pltpu.get_barrier_semaphore()

    def greet(k, carry):
        pl.semaphore_signal(barrier, inc=1, device_id={"depth": peer(k)}, device_id_type=MESH)
        return carry

    lax.fori_loop(1, n, greet, 0)
    pl.semaphore_signal(barrier, inc=1, device_id={"slab": 1 - slab}, device_id_type=MESH)
    src_copy = pltpu.make_async_copy(src_hbm, src, src_sem)
    src_copy.start()

    q_sub = lax.broadcasted_iota(I32, (requests, requests), 0)
    q_lane = lax.broadcasted_iota(I32, (requests, requests), 1)
    diag = q_sub == q_lane
    owner_col = owner_ref[...]
    owner_row = jnp.sum(jnp.where(diag, owner_col, 0), axis=0, keepdims=True)
    local_col = jnp.sum(jnp.where(diag, local_ref[...], 0).astype(F32), axis=1, keepdims=True)
    shift_col = jnp.sum(
        jnp.where(diag, shift_ref[...] + MAXSHIFT, 0).astype(F32), axis=1, keepdims=True
    )
    same = (owner_row == owner_col) & (q_lane < q_sub)
    slot_col = jnp.sum(jnp.where(same, 1.0, 0.0), axis=1, keepdims=True)
    lane = lax.broadcasted_iota(I32, (requests, cols), 1)
    row_col = lax.rem(lax.broadcasted_iota(I32, (requests, cols), 0), rows).astype(F32)
    kind = lane // cap
    value = jnp.where(
        kind == 0, local_col, jnp.where(kind == 1, shift_col, jnp.where(kind == 2, row_col, 0.0))
    )
    value = jnp.where(lax.rem(lane, cap).astype(F32) == slot_col, value, 0.0)
    owner_hot = jnp.where(
        lax.broadcasted_iota(I32, (n, requests), 0) == owner_row, 1.0, 0.0
    )
    table = jnp.dot(
        owner_hot.astype(jnp.bfloat16), value.astype(jnp.bfloat16), preferred_element_type=F32
    ).astype(I32)
    tab_send[:, 0, :] = table
    place_col = owner_col.astype(F32) * cap + slot_col
    wide_diag = lax.broadcasted_iota(I32, (requests, cols), 0) == lane
    own_v[...] = jnp.sum(jnp.where(wide_diag, place_col, 0.0), axis=0, keepdims=True).astype(I32)
    own_copy = pltpu.make_async_copy(own_v, own_s, smem_sems.at[0])
    own_copy.start()

    def push(source, target, who, number):
        return pltpu.make_async_remote_copy(
            src_ref=source, dst_ref=target, send_sem=send_sems.at[number],
            recv_sem=recv_sems.at[number], device_id=who, device_id_type=MESH,
        )

    def drain(buffer, number, sems):
        part = buffer.at[pl.ds(0, buffer.shape[0] // n * (n - 1))]
        pltpu.make_async_copy(part, part, sems.at[number]).wait()

    pl.semaphore_wait(barrier, n)

    def send_table(k, carry):
        to = peer(k)
        push(tab_send.at[to], tab_recv.at[me], {"depth": to}, 0).start()
        return carry

    lax.fori_loop(1, n, send_table, 0)
    tab_recv[me] = tab_send[me]
    ref_wide[...] = ref_ref[...].astype(F32)
    gates = jnp.concatenate([w_ref[t].astype(F32) for t in range(9)] * 2, axis=1)
    gates = gates.astype(jnp.bfloat16)
    h_eye = lax.broadcasted_iota(I32, (hidden, hidden), 0) == lax.broadcasted_iota(
        I32, (hidden, hidden), 1
    )

    def column(row):
        return jnp.sum(jnp.where(h_eye, row, 0.0), axis=1, keepdims=True)

    bias_z, bias_c, w_out = column(bz_ref[...]), column(bc_ref[...]), column(wo_ref[...])
    src_copy.wait()
    drain(tab_recv, 0, recv_sems)
    tab_copy = pltpu.make_async_copy(tab_recv, tab_s, smem_sems.at[1])
    tab_copy.start()
    tab_copy.wait()

    position = lax.broadcasted_iota(I32, (feat, cols), 1)

    def correlate(who, out, at):
        for s in range(cap):
            tile = jnp.clip(tab_s[who, 0, s], 0, src.shape[0] - 1)
            shift = jnp.clip(tab_s[who, 0, cap + s], 0, 2 * MAXSHIFT) - MAXSHIFT
            row = jnp.clip(tab_s[who, 0, 2 * cap + s], 0, rows - 1)
            wide = src[tile].astype(F32)
            moved = pltpu.roll(wide, lax.rem(shift + cols, cols), 1)
            source_col = position - shift
            inside = (source_col >= 0) & (source_col < cols)
            prod[s] = jnp.where(inside, moved, 0.0) * ref_wide[row]
            total = prod[s, pl.ds(0, groups, stride=cpg), :]
            for c in range(1, cpg):
                total = total + prod[s, pl.ds(c, groups, stride=cpg), :]
            out[at * cap + s] = total

    def answer(k, carry):
        to = peer(k)
        correlate(to, ans_send, to)
        push(
            ans_send.at[pl.ds(to * cap, cap)], ans_recv.at[pl.ds(me * cap, cap)], {"depth": to}, 1
        ).start()
        return carry

    lax.fori_loop(1, n, answer, 0)
    correlate(me, ans_recv, me)
    own_copy.wait()
    drain(ans_recv, 1, recv_sems)

    scale = 1.0 / (VIEWS * cpg)
    cost = {}
    for p in range(PD):
        for r in range(rows):
            total = None
            for v in range(VIEWS):
                place = jnp.clip(own_s[0, (p * VIEWS + v) * rows + r], 0, n * cap - 1)
                term = ans_recv[place]
                total = term if total is None else total + term
            cost[p, r] = total * scale
    for p in range(PD):
        edge_send[p] = jnp.where(slab == 0, cost[p, rows - 1], cost[p, 0])
    edge = push(edge_send, edge_recv, {"slab": 1 - slab}, 2)
    edge.start()

    glane = lax.broadcasted_iota(I32, (groups, cols), 1)
    half = 9 * groups

    def spread(p, r, x):
        for b in (-1, 0, 1):
            if b == -1:
                y = jnp.where(glane >= 1, pltpu.roll(x, 1, 1), 0.0)
            elif b == 1:
                y = jnp.where(glane < cols - 1, pltpu.roll(x, cols - 1, 1), 0.0)
            else:
                y = x
            high = y.astype(jnp.bfloat16).astype(F32)
            low = y - high
            for a in (-1, 0, 1):
                to = r - a
                if 0 <= to < rows:
                    t = (a + 1) * 3 + (b + 1)
                    at = pl.ds((p * rows + to) * cols, cols)
                    win[pl.ds(t * groups, groups), at] = high
                    win[pl.ds(half + t * groups, groups), at] = low

    for p in range(PD):
        for r in range(rows):
            spread(p, r, cost[p, r])
    edge.wait_recv()
    for p in range(PD):
        x = edge_recv[p]
        spread(p, -1, jnp.where(slab == 1, x, 0.0))
        spread(p, rows, jnp.where(slab == 0, x, 0.0))

    preact = jnp.dot(gates, win[...].astype(jnp.bfloat16), preferred_element_type=F32)
    retain = jax.nn.sigmoid(preact[:hidden] + bias_z)
    fresh = (1.0 - retain) * jnp.tanh(preact[hidden:] + bias_c)
    span = rows * cols
    decay, offset = [], []
    for p in range(PD):
        keep = retain[:, p * span : (p + 1) * span]
        new = fresh[:, p * span : (p + 1) * span]
        decay.append(keep if p == 0 else keep * decay[-1])
        offset.append(new if p == 0 else keep * offset[-1] + new)

    for r in range(rows):
        at = slice(r * cols, (r + 1) * cols)
        for j in range(hidden // seg):
            units = slice(j * seg, (j + 1) * seg)
            fwd_send[r * (hidden // seg) + j, 0:seg, :] = decay[-1][units, at]
            fwd_send[r * (hidden // seg) + j, seg : 2 * seg, :] = offset[-1][units, at]
    used = rows * hidden // seg
    if used < n:
        fwd_send[used:] = jnp.zeros((n - used, 2 * seg, cols), F32)

    def send_chunk(k, carry):
        to = peer(k)
        push(fwd_send.at[to], fwd_recv.at[me], {"depth": to}, 3).start()
        return carry

    lax.fori_loop(1, n, send_chunk, 0)
    fwd_recv[me] = fwd_send[me]
    decay_out = [w_out * x for x in decay]
    offset_out = [jnp.sum(w_out * x, axis=0, keepdims=True) for x in offset]
    drain(fwd_recv, 3, recv_sems)

    def compose(i, state):
        back_send[i] = state
        return fwd_recv[i, 0:seg, :] * state + fwd_recv[i, seg : 2 * seg, :]

    lax.fori_loop(0, n, compose, jnp.zeros((seg, cols), F32), unroll=n <= 16)

    def send_back(k, carry):
        to = peer(k)
        push(back_send.at[to], back_recv.at[me], {"depth": to}, 4).start()
        return carry

    lax.fori_loop(1, n, send_back, 0)
    back_recv[me] = back_send[me]
    drain(back_recv, 4, recv_sems)
    chunks = [back_recv[j] for j in range(used)]
    per_row = hidden // seg
    before = jnp.concatenate(
        [
            jnp.concatenate(chunks[r * per_row : (r + 1) * per_row], axis=0)
            for r in range(rows)
        ],
        axis=1,
    )

    scores = [
        jnp.sum(decay_out[p] * before, axis=0, keepdims=True) + offset_out[p] for p in range(PD)
    ]
    top = functools.reduce(jnp.maximum, scores)
    weights = [jnp.exp(s - top) for s in scores]
    total = functools.reduce(jnp.add, weights)
    values = []
    for p in range(PD):
        index = jnp.full((1, span), me * PD + p, I32).astype(F32)
        values.append(1.0 / (0.1 + 0.9 * index / (PD * n - 1)))
    weighted = functools.reduce(jnp.add, [w * v for w, v in zip(weights, values)])
    stat_send[0:1] = top
    stat_send[1:2] = total
    stat_send[2:3] = weighted

    def send_stat(k, carry):
        push(stat_send, stat_recv.at[me], {"depth": peer(k)}, 5).start()
        return carry

    lax.fori_loop(1, n, send_stat, 0)
    stat_recv[me] = stat_send[...]
    drain(stat_recv, 5, recv_sems)
    every = stat_recv[...]
    highest = jnp.max(every[:, 0:1, :], axis=0)
    share = jnp.exp(every[:, 0:1, :] - highest[None])
    totals = jnp.sum(share * every[:, 1:2, :], axis=0)
    depth_sum = jnp.sum(share * every[:, 2:3, :], axis=0)
    factor = jnp.exp(top - highest) / totals
    depth = depth_sum / totals
    for r in range(rows):
        at = slice(r * cols, (r + 1) * cols)
        depth_ref[r : r + 1, :] = depth[:, at]
        for p in range(PD):
            prob_ref[p, r : r + 1, :] = (weights[p] * factor)[:, at]

    drain(tab_send, 0, send_sems)
    drain(ans_send, 1, send_sems)
    edge.wait_send()
    drain(fwd_send, 3, send_sems)
    drain(back_send, 4, send_sems)
    drain(stat_recv, 5, send_sems)


def body(ref_feat, src_feat, tile_owner, tile_local, col_shift, w_gates, bias_z, bias_c, w_out):
    n = lax.axis_size("depth")
    rows, feat, cols = ref_feat.shape
    groups = w_gates.shape[2]
    hidden = w_gates.shape[1] // 2
    requests = tile_owner.shape[0]
    cap = max(2, (3 * requests + 2 * n - 1) // (2 * n))
    seg = max(1, rows * hidden // n)
    vmem = pl.BlockSpec(memory_space=pltpu.VMEM)
    return pl.pallas_call(
        functools.partial(kernel, n, cap, seg),
        out_shape=(
            jax.ShapeDtypeStruct((PD, rows, cols), F32),
            jax.ShapeDtypeStruct((rows, cols), F32),
        ),
        in_specs=[vmem, pl.BlockSpec(memory_space=pl.ANY)] + [vmem] * 7,
        out_specs=(vmem, vmem),
        scratch_shapes=[
            pltpu.VMEM(src_feat.shape, src_feat.dtype),
            pltpu.VMEM((rows, feat, cols), F32),
            pltpu.VMEM((n, 1, cols), I32),
            pltpu.VMEM((n, 1, cols), I32),
            pltpu.SMEM((n, 1, cols), I32),
            pltpu.VMEM((1, cols), I32),
            pltpu.SMEM((1, cols), I32),
            pltpu.VMEM((cap, feat, cols), F32),
            pltpu.VMEM((n * cap, groups, cols), F32),
            pltpu.VMEM((n * cap, groups, cols), F32),
            pltpu.VMEM((PD, groups, cols), F32),
            pltpu.VMEM((PD, groups, cols), F32),
            pltpu.VMEM((18 * groups, PD * rows * cols), F32),
            pltpu.VMEM((n, 2 * seg, cols), F32),
            pltpu.VMEM((n, 2 * seg, cols), F32),
            pltpu.VMEM((n, seg, cols), F32),
            pltpu.VMEM((n, seg, cols), F32),
            pltpu.VMEM((3, rows * cols), F32),
            pltpu.VMEM((n, 3, rows * cols), F32),
            pltpu.SemaphoreType.DMA,
            pltpu.SemaphoreType.DMA((2,)),
            pltpu.SemaphoreType.DMA((6,)),
            pltpu.SemaphoreType.DMA((6,)),
        ],
        compiler_params=pltpu.CompilerParams(
            collective_id=0, has_side_effects=True, vmem_limit_bytes=32 * 1024 * 1024
        ),
        cost_estimate=pl.CostEstimate(
            flops=2 * 144 * 64 * 1024, bytes_accessed=src_feat.size * 2, transcendentals=65536
        ),
    )(
        ref_feat, src_feat, tile_owner, tile_local.reshape(1, requests),
        col_shift.reshape(1, requests), w_gates, bias_z.reshape(1, hidden),
        bias_c.reshape(1, hidden), w_out.reshape(1, hidden),
    )


def solution(mesh):
    return jax.shard_map(
        body,
        mesh=mesh,
        in_specs=(
            P("slab", None, None),
            P("depth", None, None),
            P(("depth", "slab"), None),
            P(("depth", "slab")),
            P(("depth", "slab")),
            P(),
            P(),
            P(),
            P(),
        ),
        out_specs=(P("depth", "slab", None), P("slab", None)),
        check_vma=False,
    )
```

time: 236 us -> 41.3 us (0.17)
  blocking collectives: 155 us -> 0 us
  Pallas kernels: 0 us -> 32.2 us
  waiting for transfers between devices: 26 us -> 0 us
  starting transfers between devices: 25.9 us -> 0 us
  local copies, waits for them, and re-layouts: 19.2 us -> 8.06 us
  other arithmetic: 6.58 us -> 0 us
    all_gather x2 -> x0, blocking collectives: 79.8 us -> none  [prefix_2(): everything = jax.tree.map(lambda part: lax.all_gather(part, axis), shard)]
    pmax x1 -> x0, blocking collectives: 38.6 us -> none  [body(): highest = lax.pmax(local_max, 'depth')]
    psum x1 -> x0, blocking collectives: 36.5 us -> none  [body(): lax.psum((jnp.sum(weights, axis=0), jnp.sum(weights * depth_value[:, None...]
    pallas_call x0 -> x1, Pallas kernels: none -> 32.2 us  [body(): pl.pallas_call(functools.partial(kernel, n, cap, seg), out_shape=(jax.Sha...]
    all_to_all x4 -> x0, waiting for transfers between devices: 24.3 us -> none  [the longest x1 12.9 us: body(): lax.all_to_all(send_rows, 'depth', split_axis=0, concat_axis=0, tiled=True)]
    all_to_all x4 -> x0, starting transfers between devices: 23.3 us -> none  [the longest x1 8.31 us: body(): lax.all_to_all(send_ids, 'depth', split_axis=0, concat_axis=0, tiled=True)]
    scatter x3 -> x0, local copies, waits for them, and re-layouts: 14.5 us -> none  [the longest x1 5.57 us: body(): send_rows = jnp.zeros((owners, capacity, feat_count, col_count), jnp.bflo...]
    unnamed x18, local copies, waits for them, and re-layouts: 0.2 us -> 8.06 us
  transfers between devices with their start and end apart: 6 -> 0, of which waited for: 5 -> 0; matrix products, arithmetic and copies ran while one was open for 5% -> 0% of each run, Pallas kernels for 0% -> 0%
where the time goes in v1:
time: 41.3 us; the launch traced here: 41 us
  Pallas kernels  32.2 us (78%)
  local copies, waits for them, and re-layouts  8.06 us (20%)
  between operations  0.65 us (2%)
    pallas_call x1, Pallas kernels, body(): pl.pallas_call(functools.partial(kernel, n, cap, seg), out_shape=(jax.Sha...  32.2 us
    unnamed x18, local copies, waits for them, and re-layouts  8.06 us

profile of v1, /device:TPU:0, one launch (start us, length us, event | category | flops | bytes accessed | tf_op | source)
XLA Modules:
  0.0 41.0 jit_solution(16926830638266057798)
XLA Ops:
  0.6 0.7 %copy.11.owner_ref = s32[40,1]{1,0:T(8,128)S(1)} copy(s32[40,1]{0,1:T(1,128)} %param.11) | data formatting | bytes 320 | tf_op args[2]
  1.4 0.9 %copy.12.w_ref = bf16[9,64,8]{2,1,0:T(8,128)(2,1)S(1)} copy(bf16[9,64,8]{1,2,0:T(8,128)(2,1)} %param.14) | data formatting | bytes 18432 | tf_op args[5]
  2.2 0.0 copy-start
  2.2 1.3 %copy-done = bf16[160,32,128]{2,1,0:T(8,128)(2,1)S(1)} copy-done((bf16[160,32,128]{2,1,0:T(8,128)(2,1)S(1)}, bf16[160,32,128]{2,1,0:T(8,128)(2,1)}, u32[]{:S(2)}) %copy-start) | copy-done | bytes 1310744
  3.5 0.0 copy-start.1
  3.6 0.7 %copy-done.1 = bf16[2,32,128]{2,1,0:T(8,128)(2,1)S(1)} copy-done((bf16[2,32,128]{2,1,0:T(8,128)(2,1)S(1)}, bf16[2,32,128]{2,1,0:T(8,128)(2,1)}, u32[]{:S(2)}) %copy-start.1) | copy-done | bytes 16408
  4.3 0.0 copy-start.2
  4.3 0.7 %copy-done.2 = s32[40]{0:T(128)S(1)} copy-done((s32[40]{0:T(128)S(1)}, s32[40]{0:T(128)}, u32[]{:S(2)}) %copy-start.2) | copy-done | bytes 184
  4.9 0.0 copy-start.3
  4.9 0.7 %copy-done.3 = s32[40]{0:T(128)S(1)} copy-done((s32[40]{0:T(128)S(1)}, s32[40]{0:T(128)}, u32[]{:S(2)}) %copy-start.3) | copy-done | bytes 184
  5.6 0.0 copy-start.4
  5.6 0.7 %copy-done.4 = f32[32]{0:T(128)S(1)} copy-done((f32[32]{0:T(128)S(1)}, f32[32]{0:T(128)}, u32[]{:S(2)}) %copy-start.4) | copy-done | bytes 152
  6.2 0.0 copy-start.5
  6.2 0.7 %copy-done.5 = f32[32]{0:T(128)S(1)} copy-done((f32[32]{0:T(128)S(1)}, f32[32]{0:T(128)}, u32[]{:S(2)}) %copy-start.5) | copy-done | bytes 152
  6.9 0.0 copy-start.6
  6.9 0.7 %copy-done.6 = f32[32]{0:T(128)S(1)} copy-done((f32[32]{0:T(128)S(1)}, f32[32]{0:T(128)}, u32[]{:S(2)}) %copy-start.6) | copy-done | bytes 152
  7.5 32.2 %shard_map.104 = (f32[4,2,128]{2,1,0:T(2,128)S(1)}, f32[2,128]{1,0:T(2,128)S(1)}) custom-call(bf16[2,32,128]{2,1,0:T(8,128)(2,1)S(1)} %copy-done.1, bf16[160,32,128]{2,1,0:T(8,128)(2,1)S(1)} %copy-done, s32[40,1]{1,0:T(8,128)S(1)} %copy.11.owner_ref, s32[1,40]{1,0:T(1,128)S(1)} %bitcast.5, s32[1,40]{1,0:T(1,128)S(1)} %bitcast.6, ...), custom_call_target="tpu_custom_call" | custom-call | flops 18874368 | bytes 1310720 | tf_op jit(solution)/shard_map/pallas_call | solution.py:298
  39.8 0.6 %copy.15 = f32[4,2,128]{2,1,0:T(2,128)} copy(f32[4,2,128]{2,1,0:T(2,128)S(1)} %get-tuple-element.4) | data formatting | bytes 8192
  40.4 0.6 %copy.16 = f32[2,128]{1,0:T(2,128)} copy(f32[2,128]{1,0:T(2,128)S(1)} %get-tuple-element.5) | data formatting | bytes 2048
Async XLA Ops:
  2.2 1.3 %copy-start = (bf16[160,32,128]{2,1,0:T(8,128)(2,1)S(1)}, bf16[160,32,128]{2,1,0:T(8,128)(2,1)}, u32[]{:S(2)}) copy-start(bf16[160,32,128]{2,1,0:T(8,128)(2,1)} %src_hbm.1) | copy-start | bytes 3932164
  3.5 0.7 %copy-start.1 = (bf16[2,32,128]{2,1,0:T(8,128)(2,1)S(1)}, bf16[2,32,128]{2,1,0:T(8,128)(2,1)}, u32[]{:S(2)}) copy-start(bf16[2,32,128]{2,1,0:T(8,128)(2,1)} %ref_ref.1) | copy-start | bytes 49156
  4.3 0.7 %copy-start.2 = (s32[40]{0:T(128)S(1)}, s32[40]{0:T(128)}, u32[]{:S(2)}) copy-start(s32[40]{0:T(128)} %param.12) | copy-start | bytes 484
  4.9 0.7 %copy-start.3 = (s32[40]{0:T(128)S(1)}, s32[40]{0:T(128)}, u32[]{:S(2)}) copy-start(s32[40]{0:T(128)} %param.13) | copy-start | bytes 484
  5.6 0.7 %copy-start.4 = (f32[32]{0:T(128)S(1)}, f32[32]{0:T(128)}, u32[]{:S(2)}) copy-start(f32[32]{0:T(128)} %param.15) | copy-start | bytes 388
  6.2 0.7 %copy-start.5 = (f32[32]{0:T(128)S(1)}, f32[32]{0:T(128)}, u32[]{:S(2)}) copy-start(f32[32]{0:T(128)} %param.16) | copy-start | bytes 388
  6.9 0.7 %copy-start.6 = (f32[32]{0:T(128)S(1)}, f32[32]{0:T(128)}, u32[]{:S(2)}) copy-start(f32[32]{0:T(128)} %param.17) | copy-start | bytes 388

commit v2 on v1

--- a/solution.py
+++ b/solution.py
@@ -17,23 +17,31 @@
 
 def kernel(
     n, cap, seg,
-    ref_ref, src_hbm, owner_ref, local_ref, shift_ref, w_ref, bz_ref, bc_ref, wo_ref,
+    ref_hbm, src_hbm, owner_hbm, local_hbm, shift_hbm, w_hbm, bz_hbm, bc_hbm, wo_hbm,
     prob_ref, depth_ref,
-    src, ref_wide, tab_send, tab_recv, tab_s, own_v, own_s, prod, ans_send, ans_recv,
-    edge_send, edge_recv, win, fwd_send, fwd_recv, back_send, back_recv, stat_send, stat_recv,
-    src_sem, smem_sems, send_sems, recv_sems,
+    ref_ref, src, owner_ref, local_ref, shift_ref, w_ref, bz_ref, bc_ref, wo_ref,
+    src_wide, ref_wide, tab_send, tab_recv, tab_s, own_v, own_s, prod, ans_send, ans_recv,
+    edge_send, edge_recv, win, edge_win, fwd_send, fwd_recv, back_send, back_recv, stat_send, stat_recv,
+    in_sems, smem_sems, send_sems, recv_sems,
 ):
     me = lax.axis_index("depth")
     slab = lax.axis_index("slab")
-    requests = owner_ref.shape[0]
+    requests = owner_ref.shape[1]
     rows, feat, cols = ref_ref.shape
-    groups = w_ref.shape[2]
-    hidden = w_ref.shape[1] // 2
+    groups = w_ref.shape[1]
+    hidden = w_ref.shape[2] // 2
     cpg = feat // groups
 
     def peer(k):
         return lax.rem(me + k, n)
 
+    pairs = [
+        (owner_hbm, owner_ref), (local_hbm, local_ref), (shift_hbm, shift_ref), (ref_hbm, ref_ref),
+        (src_hbm, src), (w_hbm, w_ref), (bz_hbm, bz_ref), (bc_hbm, bc_ref), (wo_hbm, wo_ref),
+    ]
+    loads = [pltpu.make_async_copy(a, b, in_sems.at[i]) for i, (a, b) in enumerate(pairs)]
+    for load in loads:
+        load.start()
     barrier = pltpu.get_barrier_semaphore()
 
     def greet(k, carry):
@@ -42,14 +50,16 @@
 
     lax.fori_loop(1, n, greet, 0)
     pl.semaphore_signal(barrier, inc=1, device_id={"slab": 1 - slab}, device_id_type=MESH)
-    src_copy = pltpu.make_async_copy(src_hbm, src, src_sem)
-    src_copy.start()
 
     q_sub = lax.broadcasted_iota(I32, (requests, requests), 0)
     q_lane = lax.broadcasted_iota(I32, (requests, requests), 1)
     diag = q_sub == q_lane
-    owner_col = owner_ref[...]
-    owner_row = jnp.sum(jnp.where(diag, owner_col, 0), axis=0, keepdims=True)
+    for load in loads[:3]:
+        load.wait()
+    owner_row = owner_ref[...]
+    owner_col = jnp.sum(
+        jnp.where(diag, owner_row, 0).astype(F32), axis=1, keepdims=True
+    ).astype(I32)
     local_col = jnp.sum(jnp.where(diag, local_ref[...], 0).astype(F32), axis=1, keepdims=True)
     shift_col = jnp.sum(
         jnp.where(diag, shift_ref[...] + MAXSHIFT, 0).astype(F32), axis=1, keepdims=True
@@ -95,9 +105,30 @@
 
     lax.fori_loop(1, n, send_table, 0)
     tab_recv[me] = tab_send[me]
-    ref_wide[...] = ref_ref[...].astype(F32)
-    gates = jnp.concatenate([w_ref[t].astype(F32) for t in range(9)] * 2, axis=1)
-    gates = gates.astype(jnp.bfloat16)
+    for load in loads[3:]:
+        load.wait()
+
+    def regroup(source, target, count, step):
+        def some(i, carry):
+            for j in range(step):
+                prod[j] = source[i * step + j].astype(F32)
+            for j in range(step):
+                for c in range(cpg):
+                    part = prod[j, pl.ds(c, groups, stride=cpg), :]
+                    target[i * step + j, pl.ds(c * groups, groups), :] = part
+            return carry
+
+        lax.fori_loop(0, count // step, some, 0)
+
+    regroup(ref_ref, ref_wide, rows, rows)
+    regroup(src, src_wide, src.shape[0], 8)
+    gates_t = w_ref[...].astype(F32).reshape(9 * groups, 2 * hidden)
+    gates_t = jnp.concatenate([gates_t, jnp.zeros((128 - 9 * groups, 2 * hidden), F32)], axis=0)
+    gates_1 = jnp.transpose(gates_t)[:, : 9 * groups]
+    gates = jnp.concatenate([gates_1, gates_1], axis=1).astype(jnp.bfloat16)
+    side = 3 * groups
+    edge_1 = jnp.where(slab == 0, gates_1[:, 2 * side :], gates_1[:, :side])
+    edge_gates = jnp.concatenate([edge_1, edge_1], axis=1).astype(jnp.bfloat16)
     h_eye = lax.broadcasted_iota(I32, (hidden, hidden), 0) == lax.broadcasted_iota(
         I32, (hidden, hidden), 1
     )
@@ -106,28 +137,37 @@
         return jnp.sum(jnp.where(h_eye, row, 0.0), axis=1, keepdims=True)
 
     bias_z, bias_c, w_out = column(bz_ref[...]), column(bc_ref[...]), column(wo_ref[...])
-    src_copy.wait()
+    half = 9 * groups
+    for at in (0, half):
+        for p in range(PD):
+            for r, a in ((0, 0), (rows - 1, 2)):
+                win[pl.ds(at + a * side, side), pl.ds((p * rows + r) * cols, cols)] = jnp.zeros(
+                    (side, cols), F32
+                )
     drain(tab_recv, 0, recv_sems)
     tab_copy = pltpu.make_async_copy(tab_recv, tab_s, smem_sems.at[1])
     tab_copy.start()
     tab_copy.wait()
 
-    position = lax.broadcasted_iota(I32, (feat, cols), 1)
+    position = lax.broadcasted_iota(I32, (groups, cols), 1)
 
     def correlate(who, out, at):
+        tiles, shifts, picked = [], [], []
         for s in range(cap):
-            tile = jnp.clip(tab_s[who, 0, s], 0, src.shape[0] - 1)
-            shift = jnp.clip(tab_s[who, 0, cap + s], 0, 2 * MAXSHIFT) - MAXSHIFT
-            row = jnp.clip(tab_s[who, 0, 2 * cap + s], 0, rows - 1)
-            wide = src[tile].astype(F32)
-            moved = pltpu.roll(wide, lax.rem(shift + cols, cols), 1)
-            source_col = position - shift
+            tiles.append(jnp.clip(tab_s[who, 0, s], 0, src.shape[0] - 1))
+            shifts.append(jnp.clip(tab_s[who, 0, cap + s], 0, 2 * MAXSHIFT) - MAXSHIFT)
+            picked.append(jnp.clip(tab_s[who, 0, 2 * cap + s], 0, rows - 1))
+        moved = [
+            pltpu.roll(src_wide[tiles[s]], lax.rem(shifts[s] + cols, cols), 1) for s in range(cap)
+        ]
+        for s in range(cap):
+            terms = moved[s] * ref_wide[picked[s]]
+            total = terms[0:groups]
+            for c in range(1, cpg):
+                total = total + terms[c * groups : (c + 1) * groups]
+            source_col = position - shifts[s]
             inside = (source_col >= 0) & (source_col < cols)
-            prod[s] = jnp.where(inside, moved, 0.0) * ref_wide[row]
-            total = prod[s, pl.ds(0, groups, stride=cpg), :]
-            for c in range(1, cpg):
-                total = total + prod[s, pl.ds(c, groups, stride=cpg), :]
-            out[at * cap + s] = total
+            out[at * cap + s] = jnp.where(inside, total, 0.0)
 
     def answer(k, carry):
         to = peer(k)
@@ -157,37 +197,40 @@
     edge = push(edge_send, edge_recv, {"slab": 1 - slab}, 2)
     edge.start()
 
-    glane = lax.broadcasted_iota(I32, (groups, cols), 1)
-    half = 9 * groups
-
-    def spread(p, r, x):
-        for b in (-1, 0, 1):
-            if b == -1:
-                y = jnp.where(glane >= 1, pltpu.roll(x, 1, 1), 0.0)
-            elif b == 1:
-                y = jnp.where(glane < cols - 1, pltpu.roll(x, cols - 1, 1), 0.0)
-            else:
-                y = x
+    def turns(x):
+        ahead = jnp.where(position >= 1, pltpu.roll(x, 1, 1), 0.0)
+        behind = jnp.where(position < cols - 1, pltpu.roll(x, cols - 1, 1), 0.0)
+        for b, y in enumerate((ahead, x, behind)):
             high = y.astype(jnp.bfloat16).astype(F32)
-            low = y - high
-            for a in (-1, 0, 1):
-                to = r - a
-                if 0 <= to < rows:
-                    t = (a + 1) * 3 + (b + 1)
-                    at = pl.ds((p * rows + to) * cols, cols)
-                    win[pl.ds(t * groups, groups), at] = high
-                    win[pl.ds(half + t * groups, groups), at] = low
+            yield b, high, y - high
 
     for p in range(PD):
         for r in range(rows):
-            spread(p, r, cost[p, r])
+            for b, high, low in turns(cost[p, r]):
+                for a in (-1, 0, 1):
+                    if 0 <= r - a < rows:
+                        t = (a + 1) * 3 + b
+                        at = pl.ds((p * rows + r - a) * cols, cols)
+                        win[pl.ds(t * groups, groups), at] = high
+                        win[pl.ds(half + t * groups, groups), at] = low
+    inner = jnp.dot(gates, win[...].astype(jnp.bfloat16), preferred_element_type=F32)
     edge.wait_recv()
     for p in range(PD):
-        x = edge_recv[p]
-        spread(p, -1, jnp.where(slab == 1, x, 0.0))
-        spread(p, rows, jnp.where(slab == 0, x, 0.0))
-
-    preact = jnp.dot(gates, win[...].astype(jnp.bfloat16), preferred_element_type=F32)
+        for b, high, low in turns(edge_recv[p]):
+            edge_win[pl.ds(b * groups, groups), pl.ds(p * cols, cols)] = high
+            edge_win[pl.ds(side + b * groups, groups), pl.ds(p * cols, cols)] = low
+    outer = jnp.dot(edge_gates, edge_win[...].astype(jnp.bfloat16), preferred_element_type=F32)
+    pieces = []
+    for p in range(PD):
+        beside = outer[:, p * cols : (p + 1) * cols]
+        for r in range(rows):
+            piece = inner[:, (p * rows + r) * cols : (p * rows + r + 1) * cols]
+            if r == 0:
+                piece = piece + jnp.where(slab == 1, beside, 0.0)
+            if r == rows - 1:
+                piece = piece + jnp.where(slab == 0, beside, 0.0)
+            pieces.append(piece)
+    preact = jnp.concatenate(pieces, axis=1)
     retain = jax.nn.sigmoid(preact[:hidden] + bias_z)
     fresh = (1.0 - retain) * jnp.tanh(preact[hidden:] + bias_c)
     span = rows * cols
@@ -301,42 +344,52 @@
             jax.ShapeDtypeStruct((PD, rows, cols), F32),
             jax.ShapeDtypeStruct((rows, cols), F32),
         ),
-        in_specs=[vmem, pl.BlockSpec(memory_space=pl.ANY)] + [vmem] * 7,
+        in_specs=[pl.BlockSpec(memory_space=pl.ANY)] * 9,
         out_specs=(vmem, vmem),
         scratch_shapes=[
+            pltpu.VMEM(ref_feat.shape, ref_feat.dtype),
             pltpu.VMEM(src_feat.shape, src_feat.dtype),
-            pltpu.VMEM((rows, feat, cols), F32),
+            pltpu.VMEM((1, requests), I32),
+            pltpu.VMEM((1, requests), I32),
+            pltpu.VMEM((1, requests), I32),
+            pltpu.VMEM((9, groups, 2 * hidden), w_gates.dtype),
+            pltpu.VMEM((1, hidden), F32),
+            pltpu.VMEM((1, hidden), F32),
+            pltpu.VMEM((1, hidden), F32),
+            pltpu.VMEM(src_feat.shape, F32),
+            pltpu.VMEM(ref_feat.shape, F32),
             pltpu.VMEM((n, 1, cols), I32),
             pltpu.VMEM((n, 1, cols), I32),
             pltpu.SMEM((n, 1, cols), I32),
             pltpu.VMEM((1, cols), I32),
             pltpu.SMEM((1, cols), I32),
-            pltpu.VMEM((cap, feat, cols), F32),
+            pltpu.VMEM((8, feat, cols), F32),
             pltpu.VMEM((n * cap, groups, cols), F32),
             pltpu.VMEM((n * cap, groups, cols), F32),
             pltpu.VMEM((PD, groups, cols), F32),
             pltpu.VMEM((PD, groups, cols), F32),
             pltpu.VMEM((18 * groups, PD * rows * cols), F32),
+            pltpu.VMEM((6 * groups, PD * cols), F32),
             pltpu.VMEM((n, 2 * seg, cols), F32),
             pltpu.VMEM((n, 2 * seg, cols), F32),
             pltpu.VMEM((n, seg, cols), F32),
             pltpu.VMEM((n, seg, cols), F32),
             pltpu.VMEM((3, rows * cols), F32),
             pltpu.VMEM((n, 3, rows * cols), F32),
-            pltpu.SemaphoreType.DMA,
+            pltpu.SemaphoreType.DMA((9,)),
             pltpu.SemaphoreType.DMA((2,)),
             pltpu.SemaphoreType.DMA((6,)),
             pltpu.SemaphoreType.DMA((6,)),
         ],
         compiler_params=pltpu.CompilerParams(
-            collective_id=0, has_side_effects=True, vmem_limit_bytes=32 * 1024 * 1024
+            collective_id=0, has_side_effects=True, vmem_limit_bytes=60 * 1024 * 1024
         ),
         cost_estimate=pl.CostEstimate(
             flops=2 * 144 * 64 * 1024, bytes_accessed=src_feat.size * 2, transcendentals=65536
         ),
     )(
-        ref_feat, src_feat, tile_owner, tile_local.reshape(1, requests),
-        col_shift.reshape(1, requests), w_gates, bias_z.reshape(1, hidden),
+        ref_feat, src_feat, tile_owner.reshape(1, requests), tile_local.reshape(1, requests),
+        col_shift.reshape(1, requests), jnp.transpose(w_gates, (0, 2, 1)), bias_z.reshape(1, hidden),
         bias_c.reshape(1, hidden), w_out.reshape(1, hidden),
     )
 

time: 41.3 us -> 36.5 us (0.88)
  local copies, waits for them, and re-layouts: 8.06 us -> 2.48 us
  Pallas kernels: 32.2 us -> 33.2 us
    unnamed x18 -> x2, local copies, waits for them, and re-layouts: 8.06 us -> 2.48 us
    pallas_call x1, Pallas kernels: 32.2 us -> 33.2 us  [body(): pl.pallas_call(functools.partial(kernel, n, cap, seg), out_shape=(jax.Sha...]
where the time goes in v2:
time: 36.5 us; the launch traced here: 36.3 us
  Pallas kernels  33.2 us (91%)
  local copies, waits for them, and re-layouts  2.48 us (7%)
  between operations  0.64 us (2%)
    pallas_call x1, Pallas kernels, body(): pl.pallas_call(functools.partial(kernel, n, cap, seg), out_shape=(jax.Sha...  33.2 us
    unnamed x2, local copies, waits for them, and re-layouts  2.48 us

profile of v2, /device:TPU:0, one launch (start us, length us, event | category | flops | bytes accessed | tf_op | source)
XLA Modules:
  0.0 36.3 jit_solution(4847353271566928842)
XLA Ops:
  0.6 33.2 %shard_map.104 = (f32[4,2,128]{2,1,0:T(2,128)}, f32[2,128]{1,0:T(2,128)}) custom-call(bf16[2,32,128]{2,1,0:T(8,128)(2,1)} %ref_hbm.1, bf16[160,32,128]{2,1,0:T(8,128)(2,1)} %src_hbm.1, s32[1,40]{1,0:T(1,128)} %bitcast.8, s32[1,40]{1,0:T(1,128)} %bitcast.9, s32[1,40]{1,0:T(1,128)} %bitcast.10, bf16[9,8,64]{2,1,0:T(8,128)(2,1)} %bitcast.7, f32[1,32]{1,0:T(1,128)} %bitcast.11, ...), custom_call_target="tpu_custom_call" | custom-call | flops 18874368 | bytes 1310720 | tf_op jit(solution)/shard_map/pallas_call | solution.py:341
  33.8 1.3 %copy.13 = f32[4,2,128]{2,1,0:T(2,128)} copy(f32[4,2,128]{2,1,0:T(2,128)} %get-tuple-element.4) | data formatting | bytes 8192
  35.1 1.2 %copy.14 = f32[2,128]{1,0:T(2,128)} copy(f32[2,128]{1,0:T(2,128)} %get-tuple-element.5) | data formatting | bytes 2048

commit v3 on v2

v3 whole, which is shorter than its diff:
```python
import functools

import jax
import jax.numpy as jnp
from jax import lax
from jax.experimental import pallas as pl
from jax.experimental.pallas import tpu as pltpu
from jax.sharding import PartitionSpec as P

VIEWS = 5
PD = 4
MAXSHIFT = 16
MESH = pl.DeviceIdType.MESH
F32 = jnp.float32
I32 = jnp.int32


def kernel(
    n, cap,
    ref_hbm, src_hbm, owner_hbm, local_hbm, shift_hbm, w_hbm, bz_hbm, bc_hbm, wo_hbm,
    prob_ref, depth_ref,
    ref_ref, src, owner_ref, local_ref, shift_ref, w_ref, bz_ref, bc_ref, wo_ref,
    src_wide, ref_wide, tab_send, tab_recv, tab_s, own_v, own_s, prod, ans_send, ans_recv,
    gates_wide, gates, own_send, own_recv, side_send, side_recv, entry, fin_send, fin_recv,
    in_sems, smem_sems, send_sems, recv_sems,
):
    me = lax.axis_index("depth")
    slab = lax.axis_index("slab")
    requests = owner_ref.shape[1]
    rows, feat, cols = ref_ref.shape
    groups = w_ref.shape[1]
    hidden = w_ref.shape[2] // 2
    cpg = feat // groups

    edge = 8
    holders = cols // edge
    once = n <= 16

    def peer(k):
        return lax.rem(me + k, n)

    def far(j):
        step = (j + 1) // 2
        return peer(n // 2 + jnp.where(lax.rem(j, 2) == 1, -step, step))

    pairs = [
        (owner_hbm, owner_ref), (local_hbm, local_ref), (shift_hbm, shift_ref), (ref_hbm, ref_ref),
        (src_hbm, src), (w_hbm, w_ref), (bz_hbm, bz_ref), (bc_hbm, bc_ref), (wo_hbm, wo_ref),
    ]
    loads = [pltpu.make_async_copy(a, b, in_sems.at[i]) for i, (a, b) in enumerate(pairs)]
    for load in loads:
        load.start()
    barrier = pltpu.get_barrier_semaphore()

    def greet(k, carry):
        pl.semaphore_signal(barrier, inc=1, device_id={"depth": peer(k)}, device_id_type=MESH)
        return carry

    def greet_side(k, carry):
        who = {"depth": peer(k), "slab": 1 - slab}
        pl.semaphore_signal(barrier, inc=1, device_id=who, device_id_type=MESH)
        return carry

    lax.fori_loop(1, n, greet, 0, unroll=once)
    lax.fori_loop(0, n, greet_side, 0, unroll=once)

    q_sub = lax.broadcasted_iota(I32, (requests, requests), 0)
    q_lane = lax.broadcasted_iota(I32, (requests, requests), 1)
    diag = q_sub == q_lane
    for load in loads[:3]:
        load.wait()
    owner_row = owner_ref[...]
    owner_col = jnp.sum(
        jnp.where(diag, owner_row, 0).astype(F32), axis=1, keepdims=True
    ).astype(I32)
    local_col = jnp.sum(jnp.where(diag, local_ref[...], 0).astype(F32), axis=1, keepdims=True)
    shift_col = jnp.sum(
        jnp.where(diag, shift_ref[...] + MAXSHIFT, 0).astype(F32), axis=1, keepdims=True
    )
    same = (owner_row == owner_col) & (q_lane < q_sub)
    slot_col = jnp.sum(jnp.where(same, 1.0, 0.0), axis=1, keepdims=True)
    lane = lax.broadcasted_iota(I32, (requests, cols), 1)
    row_col = lax.rem(lax.broadcasted_iota(I32, (requests, cols), 0), rows).astype(F32)
    kind = lane // cap
    value = jnp.where(
        kind == 0, local_col, jnp.where(kind == 1, shift_col, jnp.where(kind == 2, row_col, 0.0))
    )
    value = jnp.where(lax.rem(lane, cap).astype(F32) == slot_col, value, 0.0)
    owner_hot = jnp.where(
        lax.broadcasted_iota(I32, (n, requests), 0) == owner_row, 1.0, 0.0
    )
    table = jnp.dot(
        owner_hot.astype(jnp.bfloat16), value.astype(jnp.bfloat16), preferred_element_type=F32
    ).astype(I32)
    tab_send[:, 0, :] = table
    place_col = owner_col.astype(F32) * cap + slot_col
    wide_diag = lax.broadcasted_iota(I32, (requests, cols), 0) == lane
    own_v[...] = jnp.sum(jnp.where(wide_diag, place_col, 0.0), axis=0, keepdims=True).astype(I32)
    own_copy = pltpu.make_async_copy(own_v, own_s, smem_sems.at[0])
    own_copy.start()

    def push(source, target, who, number):
        return pltpu.make_async_remote_copy(
            src_ref=source, dst_ref=target, send_sem=send_sems.at[number],
            recv_sem=recv_sems.at[number], device_id=who, device_id_type=MESH,
        )

    def drain(buffer, count, number, sems):
        part = buffer.at[pl.ds(0, count)]
        pltpu.make_async_copy(part, part, sems.at[number]).wait()

    pl.semaphore_wait(barrier, 2 * n - 1)

    def send_table(k, carry):
        to = far(k)
        push(tab_send.at[to], tab_recv.at[me], {"depth": to}, 0).start()
        return carry

    lax.fori_loop(0, n - 1, send_table, 0, unroll=once)
    tab_recv[me] = tab_send[me]
    for load in loads[3:]:
        load.wait()

    def regroup(source, target, count, step):
        def some(i, carry):
            for j in range(step):
                prod[j] = source[i * step + j].astype(F32)
            for j in range(step):
                for c in range(cpg):
                    part = prod[j, pl.ds(c, groups, stride=cpg), :]
                    target[i * step + j, pl.ds(c * groups, groups), :] = part
            return carry

        lax.fori_loop(0, count // step, some, 0)

    regroup(ref_ref, ref_wide, rows, rows)
    regroup(src, src_wide, src.shape[0], 8)
    taps = [w_ref[t].astype(F32) for t in range(9)]
    span = PD * rows * hidden
    plane_of = lax.broadcasted_iota(I32, (groups, span), 1) // (rows * hidden)

    def fill(at, pieces):
        for kind in range(2):
            units = slice(kind * hidden, (kind + 1) * hidden)
            part = jnp.concatenate([x[:, units] for x in pieces] * PD, axis=1)
            for p in range(PD):
                gates_wide[pl.ds(at(p), groups), pl.ds(kind * span, span)] = jnp.where(
                    plane_of == p, part, 0.0
                )

    own_rows = PD * rows * groups
    for b in range(3):
        for r in range(rows):
            fill(
                lambda p: b * cols + (p * rows + r) * groups,
                [taps[(r - to + 1) * 3 + b] for to in range(rows)],
            )
        pieces = [jnp.zeros((groups, 2 * hidden), F32) for _ in range(rows)]
        pieces[0] = pieces[0] + jnp.where(slab == 1, taps[b], 0.0)
        pieces[-1] = pieces[-1] + jnp.where(slab == 0, taps[6 + b], 0.0)
        fill(lambda p: b * cols + own_rows + p * groups, pieces)
        rest = own_rows + PD * groups
        gates_wide[pl.ds(b * cols + rest, cols - rest), :] = jnp.zeros((cols - rest, 2 * span), F32)
    gates[...] = gates_wide[...].astype(jnp.bfloat16)
    bias_z = jnp.concatenate([bz_ref[...]] * (PD * rows), axis=1)
    bias_c = jnp.concatenate([bc_ref[...]] * (PD * rows), axis=1)
    h_eye = lax.broadcasted_iota(I32, (hidden, hidden), 0) == lax.broadcasted_iota(
        I32, (hidden, hidden), 1
    )
    out_col = jnp.sum(jnp.where(h_eye, wo_ref[...], 0.0), axis=1, keepdims=True)
    out_col = jnp.concatenate([out_col] * (PD * rows), axis=0)
    unit_block = lax.broadcasted_iota(I32, (span, cols), 0) // hidden
    lane_block = lax.rem(lax.broadcasted_iota(I32, (span, cols), 1), PD * rows)
    out_wide = jnp.where(unit_block == lane_block, out_col, 0.0)
    out_high = out_wide.astype(jnp.bfloat16)
    out_low = (out_wide - out_high.astype(F32)).astype(jnp.bfloat16)
    drain(tab_recv, n - 1, 0, recv_sems)
    tab_copy = pltpu.make_async_copy(tab_recv, tab_s, smem_sems.at[1])
    tab_copy.start()
    tab_copy.wait()

    position = lax.broadcasted_iota(I32, (groups, cols), 1)

    def correlate(who, out, at):
        tiles, shifts, picked = [], [], []
        for s in range(cap):
            tiles.append(jnp.clip(tab_s[who, 0, s], 0, src.shape[0] - 1))
            shifts.append(jnp.clip(tab_s[who, 0, cap + s], 0, 2 * MAXSHIFT) - MAXSHIFT)
            picked.append(jnp.clip(tab_s[who, 0, 2 * cap + s], 0, rows - 1))
        moved = [
            pltpu.roll(src_wide[tiles[s]], lax.rem(shifts[s] + cols, cols), 1) for s in range(cap)
        ]
        for s in range(cap):
            terms = moved[s] * ref_wide[picked[s]]
            total = terms[0:groups]
            for c in range(1, cpg):
                total = total + terms[c * groups : (c + 1) * groups]
            source_col = position - shifts[s]
            inside = (source_col >= 0) & (source_col < cols)
            out[at * cap + s] = jnp.where(inside, total, 0.0)

    def answer(k, carry):
        to = far(k)
        correlate(to, ans_send, to)
        push(
            ans_send.at[pl.ds(to * cap, cap)], ans_recv.at[pl.ds(me * cap, cap)], {"depth": to}, 1
        ).start()
        return carry

    lax.fori_loop(0, n - 1, answer, 0)
    correlate(me, ans_recv, me)
    own_copy.wait()
    drain(ans_recv, cap * (n - 1), 1, recv_sems)

    scale = 1.0 / (VIEWS * cpg)
    cost = {}
    for p in range(PD):
        for r in range(rows):
            total = None
            for v in range(VIEWS):
                place = jnp.clip(own_s[0, (p * VIEWS + v) * rows + r], 0, n * cap - 1)
                term = ans_recv[place]
                total = term if total is None else total + term
            cost[p, r] = total * scale

    in_block = lax.rem(position, edge)

    def rim(x):
        left = jnp.where(position == 0, 0.0, pltpu.roll(x, 1, 1))
        right = jnp.where(position == cols - 1, 0.0, pltpu.roll(x, cols - 1, 1))
        return jnp.where(in_block == 0, left, right)

    blocks = [cost[p, r] for p in range(PD) for r in range(rows)]
    near = [jnp.where(slab == 0, cost[p, rows - 1], cost[p, 0]) for p in range(PD)]
    gap = jnp.zeros((cols // 2 - PD * groups, cols), F32)
    side = jnp.concatenate([rim(x) for x in near] + [gap] + near + [gap], axis=0)
    side_send[...] = jnp.transpose(side).reshape(holders, edge, cols)

    def send_side(k, carry):
        to = far(k) if n == holders else k
        who = {"depth": to, "slab": 1 - slab}
        push(side_send.at[to], side_recv.at[me], who, 3).start()
        return carry

    own = jnp.concatenate(blocks + [rim(x) for x in blocks], axis=0)
    own_send[...] = jnp.transpose(own).reshape(holders, edge, cols)

    def send_own(k, carry):
        to = far(k) if n == holders else k

        def go():
            push(own_send.at[to], own_recv.at[me], {"depth": to}, 2).start()

        go() if n == holders else pl.when(to != me)(go)
        return carry

    if n == holders:
        def send_both(k, carry):
            send_own(k, carry)
            return send_side(k, carry)

        lax.fori_loop(0, n - 1, send_both, 0, unroll=once)
        push(side_send.at[me], side_recv.at[me], {"depth": me, "slab": 1 - slab}, 3).start()
    else:
        lax.fori_loop(0, holders, send_own, 0)
        lax.fori_loop(0, holders, send_side, 0)

    def hold():
        own_recv[me] = own_send[me]
        drain(own_recv, n - 1, 2, recv_sems)
        drain(side_recv, n, 3, recv_sems)
        count = n * edge
        here = own_recv[...].reshape(count, cols)
        beside = side_recv[...].reshape(count, cols)
        lane = lax.broadcasted_iota(I32, (count, cols), 1)
        place = lax.rem(lax.broadcasted_iota(I32, (count, cols), 0), edge)
        lower = lane < cols // 2
        main = jnp.where(lower, here, beside)
        rims = pltpu.roll(jnp.where(lower, beside, here), cols // 2, 1)
        before = jnp.where(place == 0, rims, pltpu.roll(main, 1, 0))
        after = jnp.where(place == edge - 1, rims, pltpu.roll(main, count - 1, 0))
        window = jnp.concatenate([before, main, after], axis=1)
        high = window.astype(jnp.bfloat16)
        low = (window - high.astype(F32)).astype(jnp.bfloat16)
        weight = gates[...]
        preact = jnp.dot(high, weight, preferred_element_type=F32) + jnp.dot(
            low, weight, preferred_element_type=F32
        )
        retain = jax.nn.sigmoid(preact[:, :span] + bias_z)
        fresh = (1.0 - retain) * jnp.tanh(preact[:, span:] + bias_c)

        def planes(x):
            pair = [x[:, :cols], x[:, cols:]]
            return [pair[0], pltpu.roll(pair[0], cols // 2, 1), pair[1], pltpu.roll(pair[1], cols // 2, 1)]

        keep, new = planes(retain), planes(fresh)
        decay, offset = [keep[0]], [new[0]]
        for p in range(1, PD):
            decay.append(keep[p] * decay[-1])
            offset.append(keep[p] * offset[-1] + new[p])
        if once:
            state, entries = jnp.zeros((edge, cols), F32), []
            for i in range(n):
                entries.append(state)
                at = slice(i * edge, (i + 1) * edge)
                state = decay[-1][at] * state + offset[-1][at]
            start = jnp.concatenate(entries, axis=0)
        else:
            own_recv[...] = decay[-1].reshape(n, edge, cols)
            side_recv[...] = offset[-1].reshape(n, edge, cols)

            def compose(i, state):
                entry[i] = state
                return own_recv[i] * state + side_recv[i]

            lax.fori_loop(0, n, compose, jnp.zeros((edge, cols), F32))
            start = entry[...].reshape(count, cols)
        states = [decay[p] * start + offset[p] for p in range(PD)]
        states = jnp.concatenate(
            [
                jnp.where(lower, states[p], pltpu.roll(states[p + 1], cols // 2, 1))
                for p in range(0, PD, 2)
            ],
            axis=1,
        )
        high = states.astype(jnp.bfloat16)
        low = (states - high.astype(F32)).astype(jnp.bfloat16)
        scores = jnp.dot(low, out_high, preferred_element_type=F32) + jnp.dot(
            high, out_low, preferred_element_type=F32
        )
        scores = scores + jnp.dot(high, out_high, preferred_element_type=F32)
        scores = scores.reshape(n, edge, cols)

        def over_planes(x, combine):
            x = combine(x, pltpu.roll(x, rows, 1))
            return combine(x, pltpu.roll(x, 2 * rows, 1))

        highest = over_planes(jnp.max(scores, axis=0), jnp.maximum)
        weights = jnp.exp(scores - highest[None])
        total = over_planes(jnp.sum(weights, axis=0), jnp.add)
        shape = (n, edge, cols)
        plane = lax.rem(lax.broadcasted_iota(I32, shape, 2), PD * rows) // rows
        plane = (plane + PD * lax.broadcasted_iota(I32, shape, 0)).astype(F32)
        value = 1.0 / (0.1 + 0.9 * plane / (PD * n - 1))
        depth = over_planes(jnp.sum(weights * value, axis=0), jnp.add) / total
        first = lax.broadcasted_iota(I32, shape, 2) < PD * rows
        fin_send[...] = jnp.where(first, weights / total[None], depth[None])
        fin_recv[me] = fin_send[me]

        def send_fin(k, carry):
            to = far(k)
            push(fin_send.at[to], fin_recv.at[me], {"depth": to}, 4).start()
            return carry

        lax.fori_loop(0, n - 1, send_fin, 0, unroll=once)
        drain(fin_recv, holders - 1, 4, recv_sems)

    hold() if n == holders else pl.when(me < holders)(hold)
    if n != holders:
        @pl.when(me >= holders)
        def _():
            drain(fin_recv, holders, 4, recv_sems)

    result = jnp.transpose(fin_recv[...].reshape(cols, cols))
    for r in range(rows):
        depth_ref[r : r + 1, :] = result[PD * rows + r : PD * rows + r + 1]
        for p in range(PD):
            prob_ref[p, r : r + 1, :] = result[p * rows + r : p * rows + r + 1]

    drain(tab_send, n - 1, 0, send_sems)
    drain(ans_send, cap * (n - 1), 1, send_sems)
    drain(side_send, holders, 3, send_sems)
    if n == holders:
        drain(own_send, n - 1, 2, send_sems)
        drain(fin_send, n - 1, 4, send_sems)
    else:
        @pl.when(me < holders)
        def _():
            drain(own_send, holders - 1, 2, send_sems)
            drain(fin_send, n - 1, 4, send_sems)

        @pl.when(me >= holders)
        def _():
            drain(own_send, holders, 2, send_sems)


def hand_over(prob_in, depth_in, prob_out, depth_out, sems):
    copies = [
        pltpu.make_async_copy(prob_in, prob_out, sems.at[0]),
        pltpu.make_async_copy(depth_in, depth_out, sems.at[1]),
    ]
    for copy in copies:
        copy.start()
    for copy in copies:
        copy.wait()


def body(ref_feat, src_feat, tile_owner, tile_local, col_shift, w_gates, bias_z, bias_c, w_out):
    n = lax.axis_size("depth")
    rows, feat, cols = ref_feat.shape
    groups = w_gates.shape[2]
    hidden = w_gates.shape[1] // 2
    requests = tile_owner.shape[0]
    cap = max(2, (3 * requests + 2 * n - 1) // (2 * n))
    tiles = (n, 8, cols)
    holders = (cols // 8, 8, cols)
    span = PD * rows * hidden
    anywhere = pl.BlockSpec(memory_space=pl.ANY)
    vmem = pl.BlockSpec(memory_space=pltpu.VMEM)
    shapes = (
        jax.ShapeDtypeStruct((PD, rows, cols), F32),
        jax.ShapeDtypeStruct((rows, cols), F32),
    )
    results = pl.pallas_call(
        functools.partial(kernel, n, cap),
        out_shape=shapes,
        in_specs=[anywhere] * 9,
        out_specs=(vmem, vmem),
        scratch_shapes=[
            pltpu.VMEM(ref_feat.shape, ref_feat.dtype),
            pltpu.VMEM(src_feat.shape, src_feat.dtype),
            pltpu.VMEM((1, requests), I32),
            pltpu.VMEM((1, requests), I32),
            pltpu.VMEM((1, requests), I32),
            pltpu.VMEM((9, groups, 2 * hidden), w_gates.dtype),
            pltpu.VMEM((1, hidden), F32),
            pltpu.VMEM((1, hidden), F32),
            pltpu.VMEM((1, hidden), F32),
            pltpu.VMEM(src_feat.shape, F32),
            pltpu.VMEM(ref_feat.shape, F32),
            pltpu.VMEM((n, 1, cols), I32),
            pltpu.VMEM((n, 1, cols), I32),
            pltpu.SMEM((n, 1, cols), I32),
            pltpu.VMEM((1, cols), I32),
            pltpu.SMEM((1, cols), I32),
            pltpu.VMEM((8, feat, cols), F32),
            pltpu.VMEM((n * cap, groups, cols), F32),
            pltpu.VMEM((n * cap, groups, cols), F32),
            pltpu.VMEM((3 * cols, 2 * span), F32),
            pltpu.VMEM((3 * cols, 2 * span), jnp.bfloat16),
            pltpu.VMEM(holders, F32),
            pltpu.VMEM(tiles, F32),
            pltpu.VMEM(holders, F32),
            pltpu.VMEM(tiles, F32),
            pltpu.VMEM(tiles, F32),
            pltpu.VMEM(tiles, F32),
            pltpu.VMEM(holders, F32),
            pltpu.SemaphoreType.DMA((9,)),
            pltpu.SemaphoreType.DMA((2,)),
            pltpu.SemaphoreType.DMA((5,)),
            pltpu.SemaphoreType.DMA((5,)),
        ],
        compiler_params=pltpu.CompilerParams(
            collective_id=0, has_side_effects=True, vmem_limit_bytes=60 * 1024 * 1024
        ),
        cost_estimate=pl.CostEstimate(
            flops=2 * 144 * 64 * 1024, bytes_accessed=src_feat.size * 2, transcendentals=65536
        ),
    )(
        ref_feat, src_feat, tile_owner.reshape(1, requests), tile_local.reshape(1, requests),
        col_shift.reshape(1, requests), jnp.transpose(w_gates, (0, 2, 1)), bias_z.reshape(1, hidden),
        bias_c.reshape(1, hidden), w_out.reshape(1, hidden),
    )
    return pl.pallas_call(
        hand_over,
        out_shape=shapes,
        in_specs=[anywhere] * 2,
        out_specs=(anywhere, anywhere),
        scratch_shapes=[pltpu.SemaphoreType.DMA((2,))],
        compiler_params=pltpu.CompilerParams(vmem_limit_bytes=60 * 1024 * 1024),
    )(*results)


def solution(mesh):
    return jax.shard_map(
        body,
        mesh=mesh,
        in_specs=(
            P("slab", None, None),
            P("depth", None, None),
            P(("depth", "slab"), None),
            P(("depth", "slab")),
            P(("depth", "slab")),
            P(),
            P(),
            P(),
            P(),
        ),
        out_specs=(P("depth", "slab", None), P("slab", None)),
        check_vma=False,
    )
```

time: 36.5 us -> 33.9 us (0.929)
  local copies, waits for them, and re-layouts: 2.48 us -> 0 us
    unnamed x2 -> x0, local copies, waits for them, and re-layouts: 2.48 us -> none
    pallas_call x1 -> x2, Pallas kernels: 33.2 us -> 33.1 us  [the longest x1 31.8 us: body(): pl.pallas_call(functools.partial(kernel, n, cap), out_shape=shapes, in_sp...]
where the time goes in v3:
time: 33.9 us; the launch traced here: 33.8 us
  Pallas kernels  33.1 us (98%)
  between operations  0.64 us (2%)
    pallas_call x1, Pallas kernels, body(): pl.pallas_call(functools.partial(kernel, n, cap), out_shape=shapes, in_sp...  31.8 us
    pallas_call x1, Pallas kernels, body(): pl.pallas_call(hand_over, out_shape=shapes, in_specs=[anywhere] * 2, out_...  1.28 us

profile of v3, /device:TPU:0, one launch (start us, length us, event | category | flops | bytes accessed | tf_op | source)
XLA Modules:
  0.0 33.8 jit_solution(8723827293829820509)
XLA Ops:
  0.6 31.8 %shard_map.104 = (f32[4,2,128]{2,1,0:T(2,128)}, f32[2,128]{1,0:T(2,128)}) custom-call(bf16[2,32,128]{2,1,0:T(8,128)(2,1)} %ref_hbm.1, bf16[160,32,128]{2,1,0:T(8,128)(2,1)} %src_hbm.1, s32[1,40]{1,0:T(1,128)} %bitcast.8, s32[1,40]{1,0:T(1,128)} %bitcast.9, s32[1,40]{1,0:T(1,128)} %bitcast.10, bf16[9,8,64]{2,1,0:T(8,128)(2,1)} %bitcast.7, f32[1,32]{1,0:T(1,128)} %bitcast.11, ...), custom_call_target="tpu_custom_call" | custom-call | flops 18874368 | bytes 1310720 | tf_op jit(solution)/shard_map/pallas_call | solution.py:414
  32.5 1.3 %shard_map.105 = (f32[4,2,128]{2,1,0:T(2,128)}, f32[2,128]{1,0:T(2,128)}) custom-call(f32[4,2,128]{2,1,0:T(2,128)} %get-tuple-element.4.prob_in, f32[2,128]{1,0:T(2,128)} %get-tuple-element.5.depth_in), custom_call_target="tpu_custom_call" | custom-call | tf_op jit(solution)/shard_map/pallas_call | solution.py:464

commit v4 on v3

--- a/solution.py
+++ b/solution.py
@@ -18,10 +18,10 @@
 def kernel(
     n, cap,
     ref_hbm, src_hbm, owner_hbm, local_hbm, shift_hbm, w_hbm, bz_hbm, bc_hbm, wo_hbm,
-    prob_ref, depth_ref,
+    fin_recv,
     ref_ref, src, owner_ref, local_ref, shift_ref, w_ref, bz_ref, bc_ref, wo_ref,
-    src_wide, ref_wide, tab_send, tab_recv, tab_s, own_v, own_s, prod, ans_send, ans_recv,
-    gates_wide, gates, own_send, own_recv, side_send, side_recv, entry, fin_send, fin_recv,
+    ref_wide, tab_send, tab_recv, tab_s, own_v, own_s, prod, ans_send, ans_recv,
+    gates_wide, gates, own_send, own_recv, side_send, side_recv, entry, fin_send,
     in_sems, smem_sems, send_sems, recv_sems,
 ):
     me = lax.axis_index("depth")
@@ -118,23 +118,54 @@
 
     lax.fori_loop(0, n - 1, send_table, 0, unroll=once)
     tab_recv[me] = tab_send[me]
-    for load in loads[3:]:
+    for load in loads[3:5]:
         load.wait()
 
-    def regroup(source, target, count, step):
-        def some(i, carry):
-            for j in range(step):
-                prod[j] = source[i * step + j].astype(F32)
-            for j in range(step):
-                for c in range(cpg):
-                    part = prod[j, pl.ds(c, groups, stride=cpg), :]
-                    target[i * step + j, pl.ds(c * groups, groups), :] = part
-            return carry
-
-        lax.fori_loop(0, count // step, some, 0)
-
-    regroup(ref_ref, ref_wide, rows, rows)
-    regroup(src, src_wide, src.shape[0], 8)
+    def regroup(at):
+        return [prod[at, pl.ds(c, groups, stride=cpg), :] for c in range(cpg)]
+
+    for r in range(rows):
+        prod[r] = ref_ref[r].astype(F32)
+    for r in range(rows):
+        ref_wide[r] = jnp.concatenate(regroup(r), axis=0)
+    drain(tab_recv, n - 1, 0, recv_sems)
+    tab_copy = pltpu.make_async_copy(tab_recv, tab_s, smem_sems.at[1])
+    tab_copy.start()
+    tab_copy.wait()
+
+    position = lax.broadcasted_iota(I32, (groups, cols), 1)
+
+    def correlate(who, out, at):
+        tiles, shifts, picked = [], [], []
+        for s in range(cap):
+            tiles.append(jnp.clip(tab_s[who, 0, s], 0, src.shape[0] - 1))
+            shifts.append(jnp.clip(tab_s[who, 0, cap + s], 0, 2 * MAXSHIFT) - MAXSHIFT)
+            picked.append(jnp.clip(tab_s[who, 0, 2 * cap + s], 0, rows - 1))
+        for s in range(cap):
+            prod[s] = src[tiles[s]].astype(F32)
+        wide = [jnp.concatenate(regroup(s), axis=0) for s in range(cap)]
+        moved = [pltpu.roll(wide[s], lax.rem(shifts[s] + cols, cols), 1) for s in range(cap)]
+        for s in range(cap):
+            terms = moved[s] * ref_wide[picked[s]]
+            total = terms[0:groups]
+            for c in range(1, cpg):
+                total = total + terms[c * groups : (c + 1) * groups]
+            source_col = position - shifts[s]
+            inside = (source_col >= 0) & (source_col < cols)
+            out[at * cap + s] = jnp.where(inside, total, 0.0)
+
+    def answer(k, carry):
+        to = far(k)
+        correlate(to, ans_send, to)
+        push(
+            ans_send.at[pl.ds(to * cap, cap)], ans_recv.at[pl.ds(me * cap, cap)], {"depth": to}, 1
+        ).start()
+        return carry
+
+    lax.fori_loop(0, n - 1, answer, 0)
+    correlate(me, ans_recv, me)
+    for load in loads[5:]:
+        load.wait()
     taps = [w_ref[t].astype(F32) for t in range(9)]
     span = PD * rows * hidden
     plane_of = lax.broadcasted_iota(I32, (groups, span), 1) // (rows * hidden)
@@ -174,41 +205,6 @@
     out_wide = jnp.where(unit_block == lane_block, out_col, 0.0)
     out_high = out_wide.astype(jnp.bfloat16)
     out_low = (out_wide - out_high.astype(F32)).astype(jnp.bfloat16)
-    drain(tab_recv, n - 1, 0, recv_sems)
-    tab_copy = pltpu.make_async_copy(tab_recv, tab_s, smem_sems.at[1])
-    tab_copy.start()
-    tab_copy.wait()
-
-    position = lax.broadcasted_iota(I32, (groups, cols), 1)
-
-    def correlate(who, out, at):
-        tiles, shifts, picked = [], [], []
-        for s in range(cap):
-            tiles.append(jnp.clip(tab_s[who, 0, s], 0, src.shape[0] - 1))
-            shifts.append(jnp.clip(tab_s[who, 0, cap + s], 0, 2 * MAXSHIFT) - MAXSHIFT)
-            picked.append(jnp.clip(tab_s[who, 0, 2 * cap + s], 0, rows - 1))
-        moved = [
-            pltpu.roll(src_wide[tiles[s]], lax.rem(shifts[s] + cols, cols), 1) for s in range(cap)
-        ]
-        for s in range(cap):
-            terms = moved[s] * ref_wide[picked[s]]
-            total = terms[0:groups]
-            for c in range(1, cpg):
-                total = total + terms[c * groups : (c + 1) * groups]
-            source_col = position - shifts[s]
-            inside = (source_col >= 0) & (source_col < cols)
-            out[at * cap + s] = jnp.where(inside, total, 0.0)
-
-    def answer(k, carry):
-        to = far(k)
-        correlate(to, ans_send, to)
-        push(
-            ans_send.at[pl.ds(to * cap, cap)], ans_recv.at[pl.ds(me * cap, cap)], {"depth": to}, 1
-        ).start()
-        return carry
-
-    lax.fori_loop(0, n - 1, answer, 0)
-    correlate(me, ans_recv, me)
     own_copy.wait()
     drain(ans_recv, cap * (n - 1), 1, recv_sems)
 
@@ -282,10 +278,10 @@
         window = jnp.concatenate([before, main, after], axis=1)
         high = window.astype(jnp.bfloat16)
         low = (window - high.astype(F32)).astype(jnp.bfloat16)
-        weight = gates[...]
-        preact = jnp.dot(high, weight, preferred_element_type=F32) + jnp.dot(
-            low, weight, preferred_element_type=F32
+        both = jnp.dot(
+            jnp.concatenate([high, low], axis=0), gates[...], preferred_element_type=F32
         )
+        preact = both[:count] + both[count:]
         retain = jax.nn.sigmoid(preact[:, :span] + bias_z)
         fresh = (1.0 - retain) * jnp.tanh(preact[:, span:] + bias_c)
 
@@ -345,7 +341,8 @@
         depth = over_planes(jnp.sum(weights * value, axis=0), jnp.add) / total
         first = lax.broadcasted_iota(I32, shape, 2) < PD * rows
         fin_send[...] = jnp.where(first, weights / total[None], depth[None])
-        fin_recv[me] = fin_send[me]
+        fin_own = pltpu.make_async_copy(fin_send.at[me], fin_recv.at[me], smem_sems.at[1])
+        fin_own.start()
 
         def send_fin(k, carry):
             to = far(k)
@@ -353,6 +350,7 @@
             return carry
 
         lax.fori_loop(0, n - 1, send_fin, 0, unroll=once)
+        fin_own.wait()
         drain(fin_recv, holders - 1, 4, recv_sems)
 
     hold() if n == holders else pl.when(me < holders)(hold)
@@ -360,12 +358,6 @@
         @pl.when(me >= holders)
         def _():
             drain(fin_recv, holders, 4, recv_sems)
-
-    result = jnp.transpose(fin_recv[...].reshape(cols, cols))
-    for r in range(rows):
-        depth_ref[r : r + 1, :] = result[PD * rows + r : PD * rows + r + 1]
-        for p in range(PD):
-            prob_ref[p, r : r + 1, :] = result[p * rows + r : p * rows + r + 1]
 
     drain(tab_send, n - 1, 0, send_sems)
     drain(ans_send, cap * (n - 1), 1, send_sems)
@@ -384,15 +376,13 @@
             drain(own_send, holders, 2, send_sems)
 
 
-def hand_over(prob_in, depth_in, prob_out, depth_out, sems):
-    copies = [
-        pltpu.make_async_copy(prob_in, prob_out, sems.at[0]),
-        pltpu.make_async_copy(depth_in, depth_out, sems.at[1]),
-    ]
-    for copy in copies:
-        copy.start()
-    for copy in copies:
-        copy.wait()
+def hand_over(fin_ref, prob_ref, depth_ref):
+    planes, rows, cols = prob_ref.shape
+    result = jnp.transpose(fin_ref[...].reshape(cols, cols))
+    for r in range(rows):
+        depth_ref[r : r + 1, :] = result[planes * rows + r : planes * rows + r + 1]
+        for p in range(planes):
+            prob_ref[p, r : r + 1, :] = result[p * rows + r : p * rows + r + 1]
 
 
 def body(ref_feat, src_feat, tile_owner, tile_local, col_shift, w_gates, bias_z, bias_c, w_out):
@@ -411,11 +401,11 @@
         jax.ShapeDtypeStruct((PD, rows, cols), F32),
         jax.ShapeDtypeStruct((rows, cols), F32),
     )
-    results = pl.pallas_call(
+    landed = pl.pallas_call(
         functools.partial(kernel, n, cap),
-        out_shape=shapes,
+        out_shape=jax.ShapeDtypeStruct(holders, F32),
         in_specs=[anywhere] * 9,
-        out_specs=(vmem, vmem),
+        out_specs=anywhere,
         scratch_shapes=[
             pltpu.VMEM(ref_feat.shape, ref_feat.dtype),
             pltpu.VMEM(src_feat.shape, src_feat.dtype),
@@ -426,14 +416,13 @@
             pltpu.VMEM((1, hidden), F32),
             pltpu.VMEM((1, hidden), F32),
             pltpu.VMEM((1, hidden), F32),
-            pltpu.VMEM(src_feat.shape, F32),
             pltpu.VMEM(ref_feat.shape, F32),
             pltpu.VMEM((n, 1, cols), I32),
             pltpu.VMEM((n, 1, cols), I32),
             pltpu.SMEM((n, 1, cols), I32),
             pltpu.VMEM((1, cols), I32),
             pltpu.SMEM((1, cols), I32),
-            pltpu.VMEM((8, feat, cols), F32),
+            pltpu.VMEM((cap, feat, cols), F32),
             pltpu.VMEM((n * cap, groups, cols), F32),
             pltpu.VMEM((n * cap, groups, cols), F32),
             pltpu.VMEM((3 * cols, 2 * span), F32),
@@ -444,7 +433,6 @@
             pltpu.VMEM(tiles, F32),
             pltpu.VMEM(tiles, F32),
             pltpu.VMEM(tiles, F32),
-            pltpu.VMEM(holders, F32),
             pltpu.SemaphoreType.DMA((9,)),
             pltpu.SemaphoreType.DMA((2,)),
             pltpu.SemaphoreType.DMA((5,)),
@@ -464,11 +452,10 @@
     return pl.pallas_call(
         hand_over,
         out_shape=shapes,
-        in_specs=[anywhere] * 2,
-        out_specs=(anywhere, anywhere),
-        scratch_shapes=[pltpu.SemaphoreType.DMA((2,))],
+        in_specs=[vmem],
+        out_specs=(vmem, vmem),
         compiler_params=pltpu.CompilerParams(vmem_limit_bytes=60 * 1024 * 1024),
-    )(*results)
+    )(landed)
 
 
 def solution(mesh):

time: 33.9 us -> 33.6 us (level)
    pallas_call x2, Pallas kernels: 33.1 us -> 32.8 us  [the longest x1 31.2 us: body(): pl.pallas_call(functools.partial(kernel, n, cap), out_shape=jax.ShapeDtyp...]
where the time goes in v4:
time: 33.6 us; the launch traced here: 33.4 us
  Pallas kernels  32.8 us (98%)
  between operations  0.64 us (2%)
    pallas_call x1, Pallas kernels, body(): pl.pallas_call(functools.partial(kernel, n, cap), out_shape=jax.ShapeDtyp...  31.2 us
    pallas_call x1, Pallas kernels, body(): pl.pallas_call(hand_over, out_shape=shapes, in_specs=[vmem], out_specs=(v...  1.5 us

profile of v4, /device:TPU:0, one launch (start us, length us, event | category | flops | bytes accessed | tf_op | source)
XLA Modules:
  0.0 33.4 jit_solution(17093298848836339150)
XLA Ops:
  0.6 31.2 %shard_map.104.fin_ref = f32[16,8,128]{2,1,0:T(8,128)} custom-call(bf16[2,32,128]{2,1,0:T(8,128)(2,1)} %ref_hbm.1, bf16[160,32,128]{2,1,0:T(8,128)(2,1)} %src_hbm.1, s32[1,40]{1,0:T(1,128)} %bitcast.8, s32[1,40]{1,0:T(1,128)} %bitcast.9, s32[1,40]{1,0:T(1,128)} %bitcast.10, bf16[9,8,64]{2,1,0:T(8,128)(2,1)} %bitcast.7, f32[1,32]{1,0:T(1,128)} %bitcast.11, ...), custom_call_target="tpu_custom_call" | custom-call | flops 18874368 | bytes 1310720 | tf_op jit(solution)/shard_map/pallas_call | solution.py:404
  31.9 1.5 %shard_map.105 = (f32[4,2,128]{2,1,0:T(2,128)}, f32[2,128]{1,0:T(2,128)}) custom-call(f32[16,8,128]{2,1,0:T(8,128)} %shard_map.104.fin_ref), custom_call_target="tpu_custom_call" | custom-call | tf_op jit(solution)/shard_map/pallas_call | solution.py:452

commit v5 on v4

--- a/solution.py
+++ b/solution.py
@@ -20,7 +20,8 @@
     ref_hbm, src_hbm, owner_hbm, local_hbm, shift_hbm, w_hbm, bz_hbm, bc_hbm, wo_hbm,
     fin_recv,
     ref_ref, src, owner_ref, local_ref, shift_ref, w_ref, bz_ref, bc_ref, wo_ref,
-    ref_wide, tab_send, tab_recv, tab_s, own_v, own_s, prod, ans_send, ans_recv,
+    ref_wide, tab_send, tab_recv, tab_s, own_v, own_s, prod, code_send, code_recv,
+    scale_send, scale_recv, answers,
     gates_wide, gates, own_send, own_recv, side_send, side_recv, entry, fin_send,
     in_sems, smem_sems, send_sems, recv_sems,
 ):
@@ -135,35 +136,56 @@
 
     position = lax.broadcasted_iota(I32, (groups, cols), 1)
 
-    def correlate(who, out, at):
+    top_code = 32767.0
+
+    def correlate(whos):
+        slots = [(who, s) for who in whos for s in range(cap)]
         tiles, shifts, picked = [], [], []
-        for s in range(cap):
+        for who, s in slots:
             tiles.append(jnp.clip(tab_s[who, 0, s], 0, src.shape[0] - 1))
             shifts.append(jnp.clip(tab_s[who, 0, cap + s], 0, 2 * MAXSHIFT) - MAXSHIFT)
             picked.append(jnp.clip(tab_s[who, 0, 2 * cap + s], 0, rows - 1))
-        for s in range(cap):
-            prod[s] = src[tiles[s]].astype(F32)
-        wide = [jnp.concatenate(regroup(s), axis=0) for s in range(cap)]
-        moved = [pltpu.roll(wide[s], lax.rem(shifts[s] + cols, cols), 1) for s in range(cap)]
-        for s in range(cap):
-            terms = moved[s] * ref_wide[picked[s]]
+        for i, tile in enumerate(tiles):
+            prod[i] = src[tile].astype(F32)
+        wide = [jnp.concatenate(regroup(i), axis=0) for i in range(len(slots))]
+        moved = [pltpu.roll(x, lax.rem(y + cols, cols), 1) for x, y in zip(wide, shifts)]
+        totals = []
+        for i in range(len(slots)):
+            terms = moved[i] * ref_wide[picked[i]]
             total = terms[0:groups]
             for c in range(1, cpg):
                 total = total + terms[c * groups : (c + 1) * groups]
-            source_col = position - shifts[s]
+            source_col = position - shifts[i]
             inside = (source_col >= 0) & (source_col < cols)
-            out[at * cap + s] = jnp.where(inside, total, 0.0)
+            totals.append(jnp.where(inside, total, 0.0))
+        return [totals[i * cap : (i + 1) * cap] for i in range(len(whos))]
+
+    code_rows = cap * groups
+
+    def dispatch(to, totals):
+        codes = []
+        for s, total in enumerate(totals):
+            largest = jnp.maximum(jnp.max(jnp.abs(total), axis=0, keepdims=True), 1e-30)
+            codes.append(jnp.round(total * (top_code / largest)).astype(I32))
+            scale_send[to, s : s + 1, :] = largest * (1.0 / (top_code * VIEWS * cpg))
+        at = pl.ds(pl.multiple_of(to * code_rows, code_rows), code_rows)
+        code_send[at, :] = jnp.concatenate(codes, axis=0).astype(jnp.int16)
+        home = pl.ds(pl.multiple_of(me * code_rows, code_rows), code_rows)
+        push(code_send.at[at], code_recv.at[home], {"depth": to}, 1).start()
+        push(scale_send.at[to], scale_recv.at[me], {"depth": to}, 5).start()
 
     def answer(k, carry):
-        to = far(k)
-        correlate(to, ans_send, to)
-        push(
-            ans_send.at[pl.ds(to * cap, cap)], ans_recv.at[pl.ds(me * cap, cap)], {"depth": to}, 1
-        ).start()
-        return carry
-
-    lax.fori_loop(0, n - 1, answer, 0)
-    correlate(me, ans_recv, me)
+        pair = [far(2 * k), far(2 * k + 1)]
+        for to, totals in zip(pair, correlate(pair)):
+            dispatch(to, totals)
+        return carry
+
+    lax.fori_loop(0, (n - 1) // 2, answer, 0)
+    last = far(n - 2)
+    for_last, for_me = correlate([last, me])
+    dispatch(last, for_last)
+    for s in range(cap):
+        answers[me * cap + s] = for_me[s] * (1.0 / (VIEWS * cpg))
     for load in loads[5:]:
         load.wait()
     taps = [w_ref[t].astype(F32) for t in range(9)]
@@ -206,18 +228,28 @@
     out_high = out_wide.astype(jnp.bfloat16)
     out_low = (out_wide - out_high.astype(F32)).astype(jnp.bfloat16)
     own_copy.wait()
-    drain(ans_recv, cap * (n - 1), 1, recv_sems)
-
-    scale = 1.0 / (VIEWS * cpg)
+    drain(code_recv, code_rows * (n - 1), 1, recv_sems)
+    drain(scale_recv, n - 1, 5, recv_sems)
+
+    def decode(k, carry):
+        source = peer(k)
+        at = pl.ds(pl.multiple_of(source * code_rows, code_rows), code_rows)
+        values = code_recv[at, :].astype(I32).astype(F32)
+        for s in range(cap):
+            part = values[s * groups : (s + 1) * groups]
+            answers[source * cap + s] = part * scale_recv[source, s : s + 1, :]
+        return carry
+
+    lax.fori_loop(1, n, decode, 0, unroll=once)
     cost = {}
     for p in range(PD):
         for r in range(rows):
             total = None
             for v in range(VIEWS):
                 place = jnp.clip(own_s[0, (p * VIEWS + v) * rows + r], 0, n * cap - 1)
-                term = ans_recv[place]
+                term = answers[place]
                 total = term if total is None else total + term
-            cost[p, r] = total * scale
+            cost[p, r] = total
 
     in_block = lax.rem(position, edge)
 
@@ -339,8 +371,11 @@
         plane = (plane + PD * lax.broadcasted_iota(I32, shape, 0)).astype(F32)
         value = 1.0 / (0.1 + 0.9 * plane / (PD * n - 1))
         depth = over_planes(jnp.sum(weights * value, axis=0), jnp.add) / total
-        first = lax.broadcasted_iota(I32, shape, 2) < PD * rows
-        fin_send[...] = jnp.where(first, weights / total[None], depth[None])
+        block = lax.broadcasted_iota(I32, shape, 2) // (PD * rows)
+        column = lax.broadcasted_iota(I32, shape, 1)
+        chosen = jnp.where(block == column, weights / total[None], 0.0)
+        chosen = jnp.where(block == column + edge, depth[None], chosen)
+        fin_send[...] = jnp.sum(chosen, axis=1, keepdims=True)
         fin_own = pltpu.make_async_copy(fin_send.at[me], fin_recv.at[me], smem_sems.at[1])
         fin_own.start()
 
@@ -360,7 +395,8 @@
             drain(fin_recv, holders, 4, recv_sems)
 
     drain(tab_send, n - 1, 0, send_sems)
-    drain(ans_send, cap * (n - 1), 1, send_sems)
+    drain(code_send, code_rows * (n - 1), 1, send_sems)
+    drain(scale_send, n - 1, 5, send_sems)
     drain(side_send, holders, 3, send_sems)
     if n == holders:
         drain(own_send, n - 1, 2, send_sems)
@@ -378,9 +414,18 @@
 
 def hand_over(fin_ref, prob_ref, depth_ref):
     planes, rows, cols = prob_ref.shape
-    result = jnp.transpose(fin_ref[...].reshape(cols, cols))
+    holders = fin_ref.shape[0]
+    edge = cols // holders
+    values = jnp.broadcast_to(fin_ref[...], (holders, edge, cols)).reshape(cols, cols)
+    block = lax.broadcasted_iota(I32, (cols, cols), 1) // (planes * rows)
+    column = lax.broadcasted_iota(I32, (cols, cols), 0)
+    values = jnp.where(lax.rem(block, edge) == lax.rem(column, edge), values, 0.0)
+    turned = jnp.transpose(values)
+    half = cols // 2
+    result = turned[:half].reshape(edge, planes * rows, cols).sum(axis=0)
+    depth = turned[half:].reshape(edge, planes * rows, cols).sum(axis=0)
     for r in range(rows):
-        depth_ref[r : r + 1, :] = result[planes * rows + r : planes * rows + r + 1]
+        depth_ref[r : r + 1, :] = depth[r : r + 1]
         for p in range(planes):
             prob_ref[p, r : r + 1, :] = result[p * rows + r : p * rows + r + 1]
 
@@ -403,7 +448,7 @@
     )
     landed = pl.pallas_call(
         functools.partial(kernel, n, cap),
-        out_shape=jax.ShapeDtypeStruct(holders, F32),
+        out_shape=jax.ShapeDtypeStruct((holders[0], 1, cols), F32),
         in_specs=[anywhere] * 9,
         out_specs=anywhere,
         scratch_shapes=[
@@ -422,8 +467,11 @@
             pltpu.SMEM((n, 1, cols), I32),
             pltpu.VMEM((1, cols), I32),
             pltpu.SMEM((1, cols), I32),
-            pltpu.VMEM((cap, feat, cols), F32),
-            pltpu.VMEM((n * cap, groups, cols), F32),
+            pltpu.VMEM((2 * cap, feat, cols), F32),
+            pltpu.VMEM((n * cap * groups, cols), jnp.int16),
+            pltpu.VMEM((n * cap * groups, cols), jnp.int16),
+            pltpu.VMEM((n, cap, cols), F32),
+            pltpu.VMEM((n, cap, cols), F32),
             pltpu.VMEM((n * cap, groups, cols), F32),
             pltpu.VMEM((3 * cols, 2 * span), F32),
             pltpu.VMEM((3 * cols, 2 * span), jnp.bfloat16),
@@ -432,11 +480,11 @@
             pltpu.VMEM(holders, F32),
             pltpu.VMEM(tiles, F32),
             pltpu.VMEM(tiles, F32),
-            pltpu.VMEM(tiles, F32),
+            pltpu.VMEM((n, 1, cols), F32),
             pltpu.SemaphoreType.DMA((9,)),
             pltpu.SemaphoreType.DMA((2,)),
-            pltpu.SemaphoreType.DMA((5,)),
-            pltpu.SemaphoreType.DMA((5,)),
+            pltpu.SemaphoreType.DMA((6,)),
+            pltpu.SemaphoreType.DMA((6,)),
         ],
         compiler_params=pltpu.CompilerParams(
             collective_id=0, has_side_effects=True, vmem_limit_bytes=60 * 1024 * 1024

time: 33.6 us -> 31.3 us (0.932)
  Pallas kernels: 32.8 us -> 30.4 us
    pallas_call x1, Pallas kernels: 31.2 us -> 29.1 us  [body(): pl.pallas_call(functools.partial(kernel, n, cap), out_shape=jax.ShapeDtyp...]
where the time goes in v5:
time: 31.3 us; the launch traced here: 31.1 us
  Pallas kernels  30.4 us (97%)
  between operations  0.64 us (2%)
    pallas_call x1, Pallas kernels, body(): pl.pallas_call(functools.partial(kernel, n, cap), out_shape=jax.ShapeDtyp...  29.1 us
    pallas_call x1, Pallas kernels, body(): pl.pallas_call(hand_over, out_shape=shapes, in_specs=[vmem], out_specs=(v...  1.39 us

profile of v5, /device:TPU:0, one launch (start us, length us, event | category | flops | bytes accessed | tf_op | source)
XLA Modules:
  0.0 31.1 jit_solution(9421277370283353392)
XLA Ops:
  0.6 29.1 %shard_map.104.fin_ref = f32[16,1,128]{2,1,0:T(1,128)} custom-call(bf16[2,32,128]{2,1,0:T(8,128)(2,1)} %ref_hbm.1, bf16[160,32,128]{2,1,0:T(8,128)(2,1)} %src_hbm.1, s32[1,40]{1,0:T(1,128)} %bitcast.8, s32[1,40]{1,0:T(1,128)} %bitcast.9, s32[1,40]{1,0:T(1,128)} %bitcast.10, bf16[9,8,64]{2,1,0:T(8,128)(2,1)} %bitcast.7, f32[1,32]{1,0:T(1,128)} %bitcast.11, ...), custom_call_target="tpu_custom_call" | custom-call | flops 18874368 | bytes 1310720 | tf_op jit(solution)/shard_map/pallas_call | solution.py:449
  29.7 1.4 %shard_map.105 = (f32[4,2,128]{2,1,0:T(2,128)}, f32[2,128]{1,0:T(2,128)}) custom-call(f32[16,1,128]{2,1,0:T(1,128)} %shard_map.104.fin_ref), custom_call_target="tpu_custom_call" | custom-call | tf_op jit(solution)/shard_map/pallas_call | solution.py:500

commit v6 on v5

--- a/solution.py
+++ b/solution.py
@@ -105,6 +105,10 @@
             src_ref=source, dst_ref=target, send_sem=send_sems.at[number],
             recv_sem=recv_sems.at[number], device_id=who, device_id_type=MESH,
         )
+
+    def drain_part(buffer, count, part, number, sems):
+        got = buffer.at[pl.ds(0, count), part]
+        pltpu.make_async_copy(got, got, sems.at[number]).wait()
 
     def drain(buffer, count, number, sems):
         part = buffer.at[pl.ds(0, count)]
@@ -253,31 +257,36 @@
 
     in_block = lax.rem(position, edge)
 
-    def rim(x):
-        left = jnp.where(position == 0, 0.0, pltpu.roll(x, 1, 1))
-        right = jnp.where(position == cols - 1, 0.0, pltpu.roll(x, cols - 1, 1))
-        return jnp.where(in_block == 0, left, right)
+    def turned(x, by):
+        moved = pltpu.roll(x, by % cols, 1)
+        return jnp.where((position >= by) & (position < cols + by), moved, 0.0)
 
     blocks = [cost[p, r] for p in range(PD) for r in range(rows)]
     near = [jnp.where(slab == 0, cost[p, rows - 1], cost[p, 0]) for p in range(PD)]
-    gap = jnp.zeros((cols // 2 - PD * groups, cols), F32)
-    side = jnp.concatenate([rim(x) for x in near] + [gap] + near + [gap], axis=0)
+    side = [jnp.where(in_block < 2, x, turned(x, 3)) for x in near]
+    side += [jnp.where(in_block < 2, turned(x, -2), turned(x, -6)) for x in near]
+    side += [turned(x, -4) for x in near] + [turned(x, -6) for x in near]
+    side = jnp.concatenate(side, axis=0)
     side_send[...] = jnp.transpose(side).reshape(holders, edge, cols)
+    own_part, side_part = pl.ds(0, 5), pl.ds(0, 3)
 
     def send_side(k, carry):
         to = far(k) if n == holders else k
         who = {"depth": to, "slab": 1 - slab}
-        push(side_send.at[to], side_recv.at[me], who, 3).start()
-        return carry
-
-    own = jnp.concatenate(blocks + [rim(x) for x in blocks], axis=0)
+        push(side_send.at[to, side_part], side_recv.at[me, side_part], who, 3).start()
+        return carry
+
+    own = [jnp.where(in_block < 4, x, turned(x, 5)) for x in blocks]
+    own = jnp.concatenate(own + [turned(x, -4) for x in blocks], axis=0)
     own_send[...] = jnp.transpose(own).reshape(holders, edge, cols)
 
     def send_own(k, carry):
         to = far(k) if n == holders else k
 
         def go():
-            push(own_send.at[to], own_recv.at[me], {"depth": to}, 2).start()
+            push(
+                own_send.at[to, own_part], own_recv.at[me, own_part], {"depth": to}, 2
+            ).start()
 
         go() if n == holders else pl.when(to != me)(go)
         return carry
@@ -288,25 +297,39 @@
             return send_side(k, carry)
 
         lax.fori_loop(0, n - 1, send_both, 0, unroll=once)
-        push(side_send.at[me], side_recv.at[me], {"depth": me, "slab": 1 - slab}, 3).start()
+        send_side_me = {"depth": me, "slab": 1 - slab}
+        push(side_send.at[me, side_part], side_recv.at[me, side_part], send_side_me, 3).start()
     else:
         lax.fori_loop(0, holders, send_own, 0)
         lax.fori_loop(0, holders, send_side, 0)
 
     def hold():
         own_recv[me] = own_send[me]
-        drain(own_recv, n - 1, 2, recv_sems)
-        drain(side_recv, n, 3, recv_sems)
+        drain_part(own_recv, n - 1, own_part, 2, recv_sems)
+        drain_part(side_recv, n, side_part, 3, recv_sems)
         count = n * edge
         here = own_recv[...].reshape(count, cols)
         beside = side_recv[...].reshape(count, cols)
         lane = lax.broadcasted_iota(I32, (count, cols), 1)
         place = lax.rem(lax.broadcasted_iota(I32, (count, cols), 0), edge)
         lower = lane < cols // 2
-        main = jnp.where(lower, here, beside)
-        rims = pltpu.roll(jnp.where(lower, beside, here), cols // 2, 1)
-        before = jnp.where(place == 0, rims, pltpu.roll(main, 1, 0))
-        after = jnp.where(place == edge - 1, rims, pltpu.roll(main, count - 1, 0))
+
+        def down(x, by):
+            return pltpu.roll(x, by % count, 0)
+
+        here_2 = pltpu.roll(here, cols // 2, 1)
+        quarter = [pltpu.roll(beside, (64 - 32 * q) % cols, 1) if q != 2 else beside for q in range(4)]
+        main_1 = jnp.where(place < 4, here, down(here_2, 4))
+        main_2 = quarter[0]
+        for q in range(1, 4):
+            main_2 = jnp.where(place >= 2 * q, down(quarter[q], 2 * q), main_2)
+        main = jnp.where(lower, main_1, main_2)
+        first = jnp.where(lower, down(here, -4), down(quarter[0], -2))
+        final = jnp.where(lower, down(here_2, 3), down(quarter[1], 5))
+        before = jnp.where(place == 0, first, down(main, 1))
+        after = jnp.where(place == edge - 1, final, down(main, -1))
+        live = lane < cols // 2 + PD * groups
+        before, main, after = [jnp.where(live, x, 0.0) for x in (before, main, after)]
         window = jnp.concatenate([before, main, after], axis=1)
         high = window.astype(jnp.bfloat16)
         low = (window - high.astype(F32)).astype(jnp.bfloat16)
@@ -397,19 +420,19 @@
     drain(tab_send, n - 1, 0, send_sems)
     drain(code_send, code_rows * (n - 1), 1, send_sems)
     drain(scale_send, n - 1, 5, send_sems)
-    drain(side_send, holders, 3, send_sems)
+    drain_part(side_send, holders, side_part, 3, send_sems)
     if n == holders:
-        drain(own_send, n - 1, 2, send_sems)
+        drain_part(own_send, n - 1, own_part, 2, send_sems)
         drain(fin_send, n - 1, 4, send_sems)
     else:
         @pl.when(me < holders)
         def _():
-            drain(own_send, holders - 1, 2, send_sems)
+            drain_part(own_send, holders - 1, own_part, 2, send_sems)
             drain(fin_send, n - 1, 4, send_sems)
 
         @pl.when(me >= holders)
         def _():
-            drain(own_send, holders, 2, send_sems)
+            drain_part(own_send, holders, own_part, 2, send_sems)
 
 
 def hand_over(fin_ref, prob_ref, depth_ref):

time: 31.3 us -> 30.9 us (0.987)
  Pallas kernels: 30.4 us -> 30 us
    pallas_call x1, Pallas kernels: 29.1 us -> 28.6 us  [body(): pl.pallas_call(functools.partial(kernel, n, cap), out_shape=jax.ShapeDtyp...]
where the time goes in v6:
time: 30.9 us; the launch traced here: 30.7 us
  Pallas kernels  30 us (97%)
  between operations  0.64 us (2%)
    pallas_call x1, Pallas kernels, body(): pl.pallas_call(functools.partial(kernel, n, cap), out_shape=jax.ShapeDtyp...  28.6 us
    pallas_call x1, Pallas kernels, body(): pl.pallas_call(hand_over, out_shape=shapes, in_specs=[vmem], out_specs=(v...  1.39 us

profile of v6, /device:TPU:0, one launch (start us, length us, event | category | flops | bytes accessed | tf_op | source)
XLA Modules:
  0.0 30.7 jit_solution(18125591923705275543)
XLA Ops:
  0.6 28.6 %shard_map.104.fin_ref = f32[16,1,128]{2,1,0:T(1,128)} custom-call(bf16[2,32,128]{2,1,0:T(8,128)(2,1)} %ref_hbm.1, bf16[160,32,128]{2,1,0:T(8,128)(2,1)} %src_hbm.1, s32[1,40]{1,0:T(1,128)} %bitcast.8, s32[1,40]{1,0:T(1,128)} %bitcast.9, s32[1,40]{1,0:T(1,128)} %bitcast.10, bf16[9,8,64]{2,1,0:T(8,128)(2,1)} %bitcast.7, f32[1,32]{1,0:T(1,128)} %bitcast.11, ...), custom_call_target="tpu_custom_call" | custom-call | flops 18874368 | bytes 1310720 | tf_op jit(solution)/shard_map/pallas_call | solution.py:472
  29.3 1.4 %shard_map.105 = (f32[4,2,128]{2,1,0:T(2,128)}, f32[2,128]{1,0:T(2,128)}) custom-call(f32[16,1,128]{2,1,0:T(1,128)} %shard_map.104.fin_ref), custom_call_target="tpu_custom_call" | custom-call | tf_op jit(solution)/shard_map/pallas_call | solution.py:523

commit v7 on v6

--- a/solution.py
+++ b/solution.py
@@ -471,9 +471,9 @@
     )
     landed = pl.pallas_call(
         functools.partial(kernel, n, cap),
-        out_shape=jax.ShapeDtypeStruct((holders[0], 1, cols), F32),
+        out_shape=pltpu.VMEM((holders[0], 1, cols), F32),
         in_specs=[anywhere] * 9,
-        out_specs=anywhere,
+        out_specs=vmem,
         scratch_shapes=[
             pltpu.VMEM(ref_feat.shape, ref_feat.dtype),
             pltpu.VMEM(src_feat.shape, src_feat.dtype),
@@ -525,7 +525,6 @@
         out_shape=shapes,
         in_specs=[vmem],
         out_specs=(vmem, vmem),
-        compiler_params=pltpu.CompilerParams(vmem_limit_bytes=60 * 1024 * 1024),
     )(landed)
 
 

time: 30.9 us -> 31.5 us (1.019)
  local copies, waits for them, and re-layouts: 0 us -> 0.58 us
    unnamed x0 -> x2, local copies, waits for them, and re-layouts: none -> 0.58 us
where the time goes in v7:
time: 31.5 us; the launch traced here: 31.3 us
  Pallas kernels  30.1 us (96%)
  between operations  0.65 us (2%)
  local copies, waits for them, and re-layouts  0.58 us (2%)
    pallas_call x1, Pallas kernels, body(): pl.pallas_call(functools.partial(kernel, n, cap), out_shape=pltpu.VMEM((h...  28.7 us
    pallas_call x1, Pallas kernels, body(): pl.pallas_call(hand_over, out_shape=shapes, in_specs=[vmem], out_specs=(v...  1.38 us

profile of v7, /device:TPU:0, one launch (start us, length us, event | category | flops | bytes accessed | tf_op | source)
XLA Modules:
  0.0 31.3 jit_solution(2281040739183803436)
XLA Ops:
  0.6 28.7 %shard_map.104.fin_ref = f32[16,1,128]{2,1,0:T(1,128)S(1)} custom-call(bf16[2,32,128]{2,1,0:T(8,128)(2,1)} %ref_hbm.1, bf16[160,32,128]{2,1,0:T(8,128)(2,1)} %src_hbm.1, s32[1,40]{1,0:T(1,128)} %bitcast.8, s32[1,40]{1,0:T(1,128)} %bitcast.9, s32[1,40]{1,0:T(1,128)} %bitcast.10, bf16[9,8,64]{2,1,0:T(8,128)(2,1)} %bitcast.7, f32[1,32]{1,0:T(1,128)} %bitcast.11, ...), custom_call_target="tpu_custom_call" | custom-call | flops 18874368 | bytes 1310720 | tf_op jit(solution)/shard_map/pallas_call | solution.py:472
  29.3 0.0 copy-start
  29.3 0.6 %copy-done = f32[16,1,128]{2,1,0:T(1,128)} copy-done((f32[16,1,128]{2,1,0:T(1,128)}, f32[16,1,128]{2,1,0:T(1,128)S(1)}, u32[]{:S(2)}) %copy-start) | copy-done | bytes 8216
  29.9 1.4 %shard_map.105 = (f32[4,2,128]{2,1,0:T(2,128)}, f32[2,128]{1,0:T(2,128)}) custom-call(f32[16,1,128]{2,1,0:T(1,128)} %copy-done), custom_call_target="tpu_custom_call" | custom-call | tf_op jit(solution)/shard_map/pallas_call | solution.py:523
Async XLA Ops:
  29.3 0.6 %copy-start = (f32[16,1,128]{2,1,0:T(1,128)}, f32[16,1,128]{2,1,0:T(1,128)S(1)}, u32[]{:S(2)}) copy-start(f32[16,1,128]{2,1,0:T(1,128)S(1)} %shard_map.104.fin_ref) | copy-start | bytes 24580

commit v8 on v7

--- a/solution.py
+++ b/solution.py
@@ -525,6 +525,7 @@
         out_shape=shapes,
         in_specs=[vmem],
         out_specs=(vmem, vmem),
+        compiler_params=pltpu.CompilerParams(vmem_limit_bytes=4 * 1024 * 1024),
     )(landed)
 
 

time: 31.5 us -> 30.2 us (0.959)
  Pallas kernels: 30.1 us -> 29.4 us
  local copies, waits for them, and re-layouts: 0.58 us -> 0 us
    pallas_call x1, Pallas kernels: 1.38 us -> 0.69 us  [body(): pl.pallas_call(hand_over, out_shape=shapes, in_specs=[vmem], out_specs=(v...]
    unnamed x2 -> x0, local copies, waits for them, and re-layouts: 0.58 us -> none
where the time goes in v8:
time: 30.2 us; the launch traced here: 30 us
  Pallas kernels  29.4 us (97%)
  between operations  0.64 us (2%)
    pallas_call x1, Pallas kernels, body(): pl.pallas_call(functools.partial(kernel, n, cap), out_shape=pltpu.VMEM((h...  28.7 us
    pallas_call x1, Pallas kernels, body(): pl.pallas_call(hand_over, out_shape=shapes, in_specs=[vmem], out_specs=(v...  0.69 us

profile of v8, /device:TPU:0, one launch (start us, length us, event | category | flops | bytes accessed | tf_op | source)
XLA Modules:
  0.0 30.0 jit_solution(5321385770269132347)
XLA Ops:
  0.6 28.7 %shard_map.104.fin_ref = f32[16,1,128]{2,1,0:T(1,128)S(1)} custom-call(bf16[2,32,128]{2,1,0:T(8,128)(2,1)} %ref_hbm.1, bf16[160,32,128]{2,1,0:T(8,128)(2,1)} %src_hbm.1, s32[1,40]{1,0:T(1,128)} %bitcast.8, s32[1,40]{1,0:T(1,128)} %bitcast.9, s32[1,40]{1,0:T(1,128)} %bitcast.10, bf16[9,8,64]{2,1,0:T(8,128)(2,1)} %bitcast.7, f32[1,32]{1,0:T(1,128)} %bitcast.11, ...), custom_call_target="tpu_custom_call" | custom-call | flops 18874368 | bytes 1310720 | tf_op jit(solution)/shard_map/pallas_call | solution.py:472
  29.3 0.7 %shard_map.105 = (f32[4,2,128]{2,1,0:T(2,128)}, f32[2,128]{1,0:T(2,128)}) custom-call(f32[16,1,128]{2,1,0:T(1,128)S(1)} %shard_map.104.fin_ref), custom_call_target="tpu_custom_call" | custom-call | tf_op jit(solution)/shard_map/pallas_call | solution.py:523
